TPU v7x, 512 devices: a whole 4x8x8 slice. The times are simulated.
512 devices in a mesh: rep: 2 (over y_hi), row: 16 (over z, core), col: 16 (over x, y_lo).
Axes of the slice: x: 4, y: 8 (y_hi: 2, y_lo: 4; y = y_hi * 4 + y_lo), z: 8, core: 2. Of those that a mesh axis runs over, the one named last changes fastest.
Arguments:
- inputs: bfloat16 [512, 12288], P(('rep', 'col'), 'row'), may hold values from -6 to 6
- out_grad: bfloat16 [512, 12288], P(('rep', 'col'), 'row'), may hold values from -6 to 6
- w_in: bfloat16 [12288, 24576], P('row', ('rep', 'col')), may hold values from -0.0546875 to 0.0546875
- w_out: bfloat16 [24576, 12288], P(('rep', 'col'), 'row'), may hold values from -0.0390625 to 0.0390625
Outputs:
- grad_inputs: bfloat16 [512, 12288], P(('rep', 'col'), 'row')
- grad_w_in: bfloat16 [12288, 24576], P('row', ('rep', 'col'))
- grad_w_out: bfloat16 [24576, 12288], P(('rep', 'col'), 'row')
All inputs are finite; a program needn't handle non-finite values.
Results may differ from a plain program's by a relative error of at most 0.005.
Values may be sent and summed in bfloat16 or wider, within the bound.
No kernel may reach another device: no remote copies, remote signals or barrier semaphores. Data moves between devices by JAX's collectives and lax.ppermute only.
A program may use at most 64 MiB of HBM per device.

v0:
```python
import jax
import jax.numpy as jnp
from jax import lax
from jax.sharding import PartitionSpec as P


def gelu_tanh(value):
    return jax.nn.gelu(value, approximate=True)


def local_gelu(pre_act, back_grad):
    act_value, pullback = jax.vjp(gelu_tanh, pre_act)
    return (act_value.astype(jnp.bfloat16), pullback(back_grad)[0].astype(jnp.bfloat16))


def hidden_term(slope_rows, w_in):
    return lax.dot_general(
        slope_rows, w_in, (((1,), (1,)), ((), ())), preferred_element_type=jnp.float32
    )


def body(inputs, out_grad, w_in, w_out):
    gathered_in, gathered_grad = (
        lax.all_gather(inputs, ("rep", "col"), axis=0, tiled=True),
        lax.all_gather(out_grad, ("rep", "col"), axis=0, tiled=True),
    )
    pre_part = jnp.dot(gathered_in, w_in, preferred_element_type=jnp.float32)
    back_part = lax.dot_general(
        gathered_grad, w_out, (((1,), (1,)), ((), ())), preferred_element_type=jnp.float32
    )
    pre_act, back_grad = lax.psum((pre_part, back_part), "row")
    activation, pre_grad = local_gelu(pre_act, back_grad)
    grad_w_in = lax.dot_general(
        gathered_in, pre_grad, (((0,), (0,)), ((), ())), preferred_element_type=jnp.float32
    ).astype(jnp.bfloat16)
    grad_w_out = lax.dot_general(
        activation, gathered_grad, (((0,), (0,)), ((), ())), preferred_element_type=jnp.float32
    ).astype(jnp.bfloat16)
    grad_inputs = lax.psum_scatter(
        hidden_term(pre_grad, w_in), ("rep", "col"), scatter_dimension=0, tiled=True
    ).astype(jnp.bfloat16)
    return (grad_inputs, grad_w_in, grad_w_out)


def solution(mesh):
    placed = (
        P(("rep", "col"), "row"),
        P(("rep", "col"), "row"),
        P("row", ("rep", "col")),
        P(("rep", "col"), "row"),
    )
    return jax.shard_map(
        body,
        mesh=mesh,
        in_specs=placed,
        out_specs=(P(("rep", "col"), "row"), P("row", ("rep", "col")), P(("rep", "col"), "row")),
        check_vma=False,
    )
```

profile of v0, /device:TPU:64, one launch (start us, length us, event | category | flops | bytes accessed | tf_op | source)
XLA Modules:
  0.0 451.9 jit_solution(5317479295703750768)
XLA Ops:
  7.2 0.0 copy-start
  7.2 0.0 all-reduce.3.cloned.1.call-start
  7.2 0.0 copy-start.2
  7.2 78.9 %all_gather.7 = bf16[512,768]{1,0:T(8,128)(2,1)S(1)} all-gather(bf16[16,768]{1,0:T(8,128)(2,1)} %param.4), channel_id=1, replica_groups=mesh['rep'=2,'row'=16,'col'=16] {'rep','col'}, dimensions={0}, use_global_device_ids=true | all-gather | bytes 811008 | tf_op jit(solution)/shard_map/all_gather | solution.py:24
  86.2 72.6 %all_gather.6 = bf16[512,768]{1,0:T(8,128)(2,1)S(1)} all-gather(bf16[16,768]{1,0:T(8,128)(2,1)} %param.5), channel_id=1, replica_groups=mesh['rep'=2,'row'=16,'col'=16] {'rep','col'}, dimensions={0}, use_global_device_ids=true | all-gather | bytes 811008 | tf_op jit(solution)/shard_map/all_gather | solution.py:25
  158.7 0.0 copy-done.2
  158.7 2.0 fusion.16
  160.7 0.0 copy-done
  160.7 1.9 fusion.17
  162.6 0.0 all-reduce.3.cloned.1.call-update
  162.7 0.0 reduce-scatter.2.cloned.1.call-start
  162.7 120.4 %all-reduce.3.cloned.1.call-done = (f32[512,768]{1,0:T(8,128)}, f32[512,768]{1,0:T(8,128)}) async-done(((f32[512,768]{1,0:T(8,128)}, f32[512,768]{1,0:T(8,128)}), (f32[512,768]{1,0:T(8,128)}, f32[512,768]{1,0:T(8,128)})) %all-reduce.3.cloned.1.call-update) | async-done | bytes 3145744 | tf_op jit(solution)/shard_map/psum | solution.py:31
  283.1 2.9 fusion.6
  286.1 2.0 fusion.18
  288.0 0.0 reduce-scatter.2.cloned.1.call-update
  288.1 1.8 fusion.7
  289.9 0.0 copy-start.1
  289.9 2.5 copy.7
  292.4 0.0 copy-done.1
  292.4 2.0 convolution_convert_fusion
  294.3 149.3 %reduce-scatter.2.cloned.1.call-done = f32[16,768]{1,0:T(8,128)} async-done(((f32[512,768]{1,0:T(8,128)}), f32[16,768]{1,0:T(8,128)}) %reduce-scatter.2.cloned.1.call-update) | async-done | bytes 49168 | tf_op jit(solution)/shard_map/reduce_scatter | solution.py:39
  443.6 1.4 convert_element_type.19
Async XLA Ops:
  7.2 153.5 %copy-start = (bf16[768,768]{1,0:T(8,128)(2,1)S(1)}, bf16[768,768]{1,0:T(8,128)(2,1)}, u32[]{:S(2)}) copy-start(bf16[768,768]{1,0:T(8,128)(2,1)} %param.6) | copy-start | bytes 3538948
  7.2 276.0 %all-reduce.3.cloned.1.call-start = ((), (), s32[]{:S(2)}) async-start(), calls=%async_computation.2 | async-start | bytes 6291456 | tf_op jit(solution)/shard_map/psum | solution.py:31
  7.2 151.5 %copy-start.2 = (bf16[768,768]{1,0:T(8,128)(2,1)S(1)}, bf16[768,768]{1,0:T(8,128)(2,1)}, u32[]{:S(2)}) copy-start(bf16[768,768]{1,0:T(8,128)(2,1)} %param.7) | copy-start | bytes 3538948
  162.7 281.0 %reduce-scatter.2.cloned.1.call-start = ((), (), s32[]{:S(2)}) async-start(), calls=%async_computation.1 | async-start | bytes 1622016 | tf_op jit(solution)/shard_map/reduce_scatter | solution.py:39
  289.9 2.5 copy-start.1
Sparse Core Ops, SparseCore 0:
  162.8 120.3 all-reduce.2
  288.2 155.4 reduce-scatter.1
where the time goes:
time: 452 us
  waiting for transfers between devices  270 us (60%)
  blocking collectives  151 us (33%)
  between operations  14.1 us (3%)
  matrix products  9.65 us (2%)
    reduce_scatter x1, waiting for transfers between devices, body(): lax.psum_scatter(hidden_term(pre_grad, w_in), ('rep', 'col'), scatter_dim...  149 us
    psum x1, waiting for transfers between devices, body(): pre_act, back_grad = lax.psum((pre_part, back_part), 'row')  120 us
    all_gather x1, blocking collectives, body(): lax.all_gather(inputs, ('rep', 'col'), axis=0, tiled=True)  78.9 us
    all_gather x1, blocking collectives, body(): lax.all_gather(out_grad, ('rep', 'col'), axis=0, tiled=True)  72.6 us
  transfers between devices with their start and end apart: 2, of which 2 were waited for; matrix products, arithmetic and copies ran while one was open for 1% of the time, Pallas kernels for 0%

commit v1 on v0

v1 whole, which is shorter than its diff:
```python
import jax
import jax.numpy as jnp
from jax import lax
from jax.sharding import Mesh
from jax.sharding import PartitionSpec as P

PLANE = ("x", "y_hi", "y_lo")
SIDE = ("y_hi", "y_lo")
ROW = ("z", "core")
SWAP = [(0, 1), (1, 0)]


def gelu_tanh(value):
    return jax.nn.gelu(value, approximate=True)


def spread(block, axes, count):
    copies = jnp.broadcast_to(block[None], (count,) + block.shape)
    return lax.all_to_all(copies, axes, 0, 0, tiled=True)


def dot(left, right, dims, out=jnp.float32):
    return lax.dot_general(
        left, right, (dims, ((), ())), preferred_element_type=jnp.float32
    ).astype(out)


def body(inputs, out_grad, w_in, w_out):
    bf16, f32 = jnp.bfloat16, jnp.float32
    feat, hid = w_in.shape
    rows = inputs.shape[0]
    half = hid // 2
    core = lax.axis_index("core")
    mine, other = core * half, (1 - core) * half

    with jax.named_scope("gather_tokens"):
        by_y = spread(jnp.stack([inputs, out_grad]), SIDE, 8)
        by_y = by_y.transpose(1, 0, 2, 3).reshape(2, 8 * rows, feat)
        by_x = spread(by_y, "x", 4)
        tokens = 32 * rows
        all_in = by_x[:, 0].reshape(tokens, feat)
        all_grad = by_x[:, 1].reshape(tokens, feat)

    w_in_other = lax.dynamic_slice(w_in, (0, other), (feat, half))
    w_in_mine = lax.dynamic_slice(w_in, (0, mine), (feat, half))
    w_out_other = lax.dynamic_slice(w_out, (other, 0), (half, feat))
    w_out_mine = lax.dynamic_slice(w_out, (mine, 0), (half, feat))

    with jax.named_scope("chip_sum"):
        sent = jnp.stack(
            [
                dot(all_in, w_in_other, ((1,), (1 - 1,)), bf16),
                dot(all_grad, w_out_other, ((1,), (1,)), bf16),
            ]
        )
        got = lax.ppermute(sent, "core", SWAP)
        pre_chip = dot(all_in, w_in_mine, ((1,), (0,))) + got[0].astype(f32)
        back_chip = dot(all_grad, w_out_mine, ((1,), (1,))) + got[1].astype(f32)

    with jax.named_scope("row_sum"):
        share = tokens // 16
        parts = jnp.stack(
            [
                pre_chip.astype(bf16).reshape(16, share, half),
                back_chip.astype(bf16).reshape(16, share, half),
            ],
            axis=1,
        )
        parts = lax.all_to_all(parts, ROW, 0, 0, tiled=True)
        sums = parts.reshape(8, 2, 2, share, half).astype(f32).sum(axis=0)
        pre_act = jnp.concatenate([sums[0, 0], sums[1, 0]], axis=1)
        back_grad = jnp.concatenate([sums[0, 1], sums[1, 1]], axis=1)

    act_value, pullback = jax.vjp(gelu_tanh, pre_act)
    activation = act_value.astype(bf16)
    pre_grad = pullback(back_grad)[0].astype(bf16)

    pre_grad = lax.all_gather(pre_grad, ROW, axis=0, tiled=True)
    with jax.named_scope("token_sum"):
        terms = dot(pre_grad, w_in, ((1,), (1,)), bf16).reshape(32, rows, feat)
        terms = lax.all_to_all(terms, PLANE, 0, 0, tiled=True)
        grad_inputs = terms.astype(f32).sum(axis=0).astype(bf16)

    activation = lax.all_gather(activation, ROW, axis=0, tiled=True)
    grad_w_in = dot(all_in, pre_grad, ((0,), (0,)), bf16)
    grad_w_out = dot(activation, all_grad, ((0,), (0,)), bf16)
    return (grad_inputs, grad_w_in, grad_w_out)


def solution(mesh):
    fine = Mesh(mesh.devices.reshape(2, 8, 2, 4, 4), ("y_hi", "z", "core", "x", "y_lo"))
    plane = ("y_hi", "x", "y_lo")
    token_block, up_block, down_block = P(plane, ROW), P(ROW, plane), P(plane, ROW)
    return jax.shard_map(
        body,
        mesh=fine,
        in_specs=(token_block, token_block, up_block, down_block),
        out_specs=(token_block, up_block, down_block),
        check_vma=False,
    )
```

time: 452 us -> 139 us (0.31)
  the two profiles are of different devices: /device:TPU:64 before, /device:TPU:1 now
where the time goes in v1:
time: 139 us; the launch traced here: 138 us
  blocking collectives  87.7 us (63%)
  waiting for transfers between devices  20.2 us (15%)
  starting transfers between devices  14.3 us (10%)
  matrix products  9.9 us (7%)
  local copies, waits for them, and re-layouts  2.89 us (2%)
  other arithmetic  2.56 us (2%)
    all_to_all x1, blocking collectives, body(): parts = lax.all_to_all(parts, ROW, 0, 0, tiled=True)  33.4 us
    all_to_all x1, blocking collectives, spread(): return lax.all_to_all(copies, axes, 0, 0, tiled=True)  19.8 us
    all_to_all x1, waiting for transfers between devices, spread(): return lax.all_to_all(copies, axes, 0, 0, tiled=True)  18.3 us
    all_gather x1, blocking collectives, body(): activation = lax.all_gather(activation, ROW, axis=0, tiled=True)  17.9 us
    all_gather x1, blocking collectives, body(): pre_grad = lax.all_gather(pre_grad, ROW, axis=0, tiled=True)  16.6 us
    dot_general x7, matrix products, dot(): lax.dot_general(left, right, (dims, ((), ())), preferred_element_type=jnp...  9.9 us
    ppermute x1, starting transfers between devices, body(): got = lax.ppermute(sent, 'core', SWAP)  5.23 us
    all_to_all x1, starting transfers between devices, spread(): return lax.all_to_all(copies, axes, 0, 0, tiled=True)  5.18 us
  transfers between devices with their start and end apart: 3, of which 2 were waited for; matrix products, arithmetic and copies ran while one was open for 3% of the time, Pallas kernels for 0%

profile of v1, /device:TPU:1, one launch (start us, length us, event | category | flops | bytes accessed | tf_op | source)
XLA Modules:
  0.0 138.4 jit_solution(3846330092336352061)
XLA Ops:
  0.6 0.0 copy-start
  0.6 0.9 pad_maximum_fusion.4
  1.5 19.8 %all_to_all.20 = bf16[8,2,16,768]{3,2,1,0:T(8,128)(2,1)S(1)} all-to-all(bf16[8,2,16,768]{3,2,1,0:T(8,128)(2,1)S(1)} %broadcast_in_dim.6), channel_id=1, replica_groups=mesh['y_hi'=2,'z'=8,'core'=2,'x'=4,'y_lo'=4] {'y_hi','y_lo'}, dimensions={0} | all-to-all | bytes 786432 | tf_op jit(solution)/shard_map/gather_tokens/all_to_all | solution.py:19
  21.4 1.3 broadcast_in_dim.15
  22.6 5.2 %all-to-all-start.1 = ((bf16[4,2,128,768]{3,2,1,0:T(8,128)(2,1)}), bf16[4,2,128,768]{3,2,1,0:T(8,128)(2,1)S(1)}, u32[]{:S(2)}, u32[]{:S(2)}) async-start(bf16[4,2,128,768]{3,2,1,0:T(8,128)(2,1)} %broadcast_in_dim.15), calls=%async_computation.1 | async-start | bytes 3145728 | tf_op jit(solution)/shard_map/gather_tokens/all_to_all | solution.py:19
  27.8 18.3 %all-to-all-done.1 = bf16[4,2,128,768]{3,2,1,0:T(8,128)(2,1)S(1)} async-done(((bf16[4,2,128,768]{3,2,1,0:T(8,128)(2,1)}), bf16[4,2,128,768]{3,2,1,0:T(8,128)(2,1)S(1)}, u32[]{:S(2)}, u32[]{:S(2)}) %all-to-all-start.1) | async-done | bytes 1572896 | tf_op jit(solution)/shard_map/gather_tokens/all_to_all | solution.py:19
  46.1 0.1 fusion.25
  46.2 0.0 copy-start.1
  46.3 1.4 %copy-done.4 = bf16[768,768]{1,0:T(8,128)(2,1)S(1)} copy-done((bf16[768,768]{1,0:T(8,128)(2,1)S(1)}, bf16[768,768]{1,0:T(8,128)(2,1)}, u32[]{:S(2)}) %copy-start.4) | copy-done | bytes 1179672
  47.7 0.6 fusion.1
  48.3 0.0 copy-done
  48.3 0.6 fusion
  48.9 0.0 copy-done.1
  48.9 0.1 pad_maximum_fusion
  49.0 5.2 %collective-permute-start = (bf16[2,512,384]{2,1,0:T(8,128)(2,1)S(1)}, bf16[2,512,384]{2,1,0:T(8,128)(2,1)S(1)}, u32[]{:S(2)}, u32[]{:S(2)}) collective-permute-start(bf16[2,512,384]{2,1,0:T(8,128)(2,1)S(1)} %pad_maximum_fusion), channel_id=1, source_target_pairs={{0,16},{16,0},{1,17},{17,1},{2,18},{18,2},{3,19},{19,3},{4,20},{20... | collective-permute-start | bytes 2359304 | tf_op jit(solution)/shard_map/chip_sum/ppermute | solution.py:56
  54.2 0.0 copy-start.2
  54.3 1.9 %collective-permute-done = bf16[2,512,384]{2,1,0:T(8,128)(2,1)S(1)} collective-permute-done((bf16[2,512,384]{2,1,0:T(8,128)(2,1)S(1)}, bf16[2,512,384]{2,1,0:T(8,128)(2,1)S(1)}, u32[]{:S(2)}, u32[]{:S(2)}) %collective-permute-start) | collective-permute-done | bytes 786464 | tf_op jit(solution)/shard_map/chip_sum/ppermute | solution.py:56
  56.1 1.7 %fusion.2 = bf16[512,384]{1,0:T(8,128)(2,1)S(1)} fusion(bf16[2,512,384]{2,1,0:T(8,128)(2,1)S(1)} %collective-permute-done, bf16[512,768]{1,0:T(8,128)(2,1)S(1)} %bitcast.65, bf16[768,768]{1,0:T(8,128)(2,1)} %param.7, s32[]{:T(128)S(6)} %select_n.8), kind=kOutput, calls=%fused_computation.11 | convolution fusion | flops 302579712 | bytes 2162692 | tf_op jit(solution)/shard_map/chip_sum/dot_general | solution.py:23
  57.8 0.6 fusion.3
  58.4 0.1 pad_maximum_fusion.1
  58.5 33.4 %all_to_all.21 = bf16[16,2,32,384]{3,2,1,0:T(8,128)(2,1)S(1)} all-to-all(bf16[16,2,32,384]{3,2,1,0:T(8,128)(2,1)S(1)} %pad_maximum_fusion.1), channel_id=1, replica_groups=mesh['y_hi'=2,'z'=8,'core'=2,'x'=4,'y_lo'=4] {'z','core'}, dimensions={0} | all-to-all | bytes 1572864 | tf_op jit(solution)/shard_map/row_sum/all_to_all | solution.py:69
  91.9 0.1 convert_reduce_fusion
  92.1 0.7 multiply_convert_fusion
  92.8 16.6 %all_gather.6 = bf16[512,768]{1,0:T(8,128)(2,1)S(1)} all-gather(bf16[32,768]{1,0:T(8,128)(2,1)S(1)} %get-tuple-element.10), channel_id=1, replica_groups=mesh['y_hi'=2,'z'=8,'core'=2,'x'=4,'y_lo'=4] {'z','core'}, dimensions={0}, use_global_device_ids=true | all-gather | bytes 835584 | tf_op jit(solution)/shard_map/all_gather | solution.py:78
  109.4 1.7 %convolution_convert_fusion.2 = bf16[512,768]{1,0:T(8,128)(2,1)} fusion(bf16[512,768]{1,0:T(8,128)(2,1)S(1)} %all_gather.6, bf16[768,768]{1,0:T(8,128)(2,1)S(1)} %copy-done), kind=kOutput, calls=%fused_computation.3 | convolution fusion | flops 604372992 | bytes 2752512 | tf_op jit(solution)/shard_map/token_sum/dot_general | solution.py:23
  111.0 3.9 %all-to-all-start.3 = ((bf16[32,16,768]{2,1,0:T(8,128)(2,1)}), bf16[32,16,768]{2,1,0:T(8,128)(2,1)S(1)}, u32[]{:S(2)}, u32[]{:S(2)}) async-start(bf16[32,16,768]{2,1,0:T(8,128)(2,1)} %bitcast.19), calls=%async_computation.3 | async-start | bytes 1572864 | tf_op jit(solution)/shard_map/token_sum/all_to_all | solution.py:81
  115.0 0.0 copy-start.3
  115.0 3.0 %convolution_convert_fusion.1 = bf16[768,768]{1,0:T(8,128)(2,1)} fusion(bf16[512,768]{1,0:T(8,128)(2,1)} %bitcast.68, bf16[512,768]{1,0:T(8,128)(2,1)S(1)} %all_gather.6), kind=kOutput, calls=%fused_computation.2 | convolution fusion | flops 604569600 | bytes 2752512 | tf_op jit(solution)/shard_map/dot_general | solution.py:23
  117.9 17.9 %all_gather.7 = bf16[512,768]{1,0:T(8,128)(2,1)S(1)} all-gather(bf16[32,768]{1,0:T(8,128)(2,1)S(1)} %copy-done.3), channel_id=1, replica_groups=mesh['y_hi'=2,'z'=8,'core'=2,'x'=4,'y_lo'=4] {'z','core'}, dimensions={0}, use_global_device_ids=true | all-gather | bytes 835584 | tf_op jit(solution)/shard_map/all_gather | solution.py:84
  135.8 1.8 %convolution_convert_fusion = bf16[768,768]{1,0:T(8,128)(2,1)} fusion(bf16[512,768]{1,0:T(8,128)(2,1)S(1)} %all_gather.7, bf16[512,768]{1,0:T(8,128)(2,1)S(1)} %bitcast.66), kind=kOutput, calls=%fused_computation.1 | convolution fusion | flops 604569600 | bytes 2752512 | tf_op jit(solution)/shard_map/dot_general | solution.py:23
  137.6 0.0 all-to-all-done.3
  137.6 0.7 reduce_sum.22
  (6 shorter events, 0.1 us)
Async XLA Ops:
  0.6 47.7 %copy-start = (bf16[768,768]{1,0:T(8,128)(2,1)S(1)}, bf16[768,768]{1,0:T(8,128)(2,1)}, u32[]{:S(2)}) copy-start(bf16[768,768]{1,0:T(8,128)(2,1)} %param.6) | copy-start | bytes 3538948
  22.6 23.5 %all-to-all-start.1 = ((bf16[4,2,128,768]{3,2,1,0:T(8,128)(2,1)}), bf16[4,2,128,768]{3,2,1,0:T(8,128)(2,1)S(1)}, u32[]{:S(2)}, u32[]{:S(2)}) async-start(bf16[4,2,128,768]{3,2,1,0:T(8,128)(2,1)} %broadcast_in_dim.15), calls=%async_computation.1 | async-start | bytes 3145728 | tf_op jit(solution)/shard_map/gather_tokens/all_to_all | solution.py:19
  46.1 1.6 %copy-start.4 = (bf16[768,768]{1,0:T(8,128)(2,1)S(1)}, bf16[768,768]{1,0:T(8,128)(2,1)}, u32[]{:S(2)}) copy-start(bf16[768,768]{1,0:T(8,128)(2,1)} %param.7) | copy-start | bytes 3538948
  46.2 2.6 %copy-start.1 = (bf16[4,1,128,768]{3,2,1,0:T(8,128)(2,1)}, bf16[4,1,128,768]{3,2,1,0:T(8,128)(2,1)S(1)}, u32[]{:S(2)}) copy-start(bf16[4,1,128,768]{3,2,1,0:T(8,128)(2,1)S(1)} %get-tuple-element.3) | copy-start | bytes 2359300
  49.0 7.1 %collective-permute-start = (bf16[2,512,384]{2,1,0:T(8,128)(2,1)S(1)}, bf16[2,512,384]{2,1,0:T(8,128)(2,1)S(1)}, u32[]{:S(2)}, u32[]{:S(2)}) collective-permute-start(bf16[2,512,384]{2,1,0:T(8,128)(2,1)S(1)} %pad_maximum_fusion), channel_id=1, source_target_pairs={{0,16},{16,0},{1,17},{17,1},{2,18},{18,2},{3,19},{19,3},{4,20},{20... | collective-permute-start | bytes 2359304 | tf_op jit(solution)/shard_map/chip_sum/ppermute | solution.py:56
  54.2 3.5 %copy-start.2 = (bf16[4,1,128,768]{3,2,1,0:T(8,128)(2,1)S(1)}, bf16[4,1,128,768]{3,2,1,0:T(8,128)(2,1)}, u32[]{:S(2)}) copy-start(bf16[4,1,128,768]{3,2,1,0:T(8,128)(2,1)} %copy-done.1) | copy-start | bytes 2359300
  111.0 26.6 %all-to-all-start.3 = ((bf16[32,16,768]{2,1,0:T(8,128)(2,1)}), bf16[32,16,768]{2,1,0:T(8,128)(2,1)S(1)}, u32[]{:S(2)}, u32[]{:S(2)}) async-start(bf16[32,16,768]{2,1,0:T(8,128)(2,1)} %bitcast.19), calls=%async_computation.3 | async-start | bytes 1572864 | tf_op jit(solution)/shard_map/token_sum/all_to_all | solution.py:81
  115.0 3.0 %copy-start.3 = (bf16[32,768]{1,0:T(8,128)(2,1)S(1)}, bf16[32,768]{1,0:T(8,128)(2,1)}, u32[]{:S(2)}) copy-start(bf16[32,768]{1,0:T(8,128)(2,1)} %get-tuple-element.9) | copy-start | bytes 147460

commit v2 on v1

v2 whole, which is shorter than its diff:
```python
import jax
import jax.numpy as jnp
from jax import lax
from jax.experimental import pallas as pl
from jax.experimental.pallas import tpu as pltpu
from jax.sharding import Mesh
from jax.sharding import PartitionSpec as P

PLANE = ("x", "y_hi", "y_lo")
SIDE = ("y_hi", "y_lo", "core")
ROW = ("z", "core")
SWAP = [(0, 1), (1, 0)]


def gelu_tanh(value):
    return jax.nn.gelu(value, approximate=True)


def dot(left, right, dims, out=jnp.float32):
    return lax.dot_general(
        left, right, (dims, ((), ())), preferred_element_type=jnp.float32
    ).astype(out)


def terms_kernel(core, tokens, w_in, w_in_swap, w_out, w_out_swap, terms):
    near, far = core[0], 1 - core[0]
    count = tokens.shape[0] * tokens.shape[3]

    def lhs(side, kind):
        return tokens[:, side, kind].reshape(count, tokens.shape[4])

    pre = dot(lhs(near, 0), w_in[...], ((1,), (0,)))
    pre += dot(lhs(far, 0), w_in_swap[...], ((1,), (0,)))
    back = dot(lhs(near, 1), w_out[...], ((1,), (1,)))
    back += dot(lhs(far, 1), w_out_swap[...], ((1,), (1,)))
    for kind, value in enumerate((pre, back)):
        terms[:, kind] = value.astype(terms.dtype).reshape(16, count // 16, value.shape[1])


def chip_terms(core, tokens, w_in, w_in_swap, w_out, w_out_swap):
    feat, hid = w_in.shape
    block = 256
    count = tokens.shape[0] * tokens.shape[3]
    up = pl.BlockSpec((feat, block), lambda j, core: (0, j))
    down = pl.BlockSpec((block, feat), lambda j, core: (j, 0))
    return pl.pallas_call(
        terms_kernel,
        grid_spec=pltpu.PrefetchScalarGridSpec(
            num_scalar_prefetch=1,
            grid=(hid // block,),
            in_specs=[
                pl.BlockSpec(tokens.shape, lambda j, core: (0,) * 5),
                up,
                up,
                down,
                down,
            ],
            out_specs=pl.BlockSpec((16, 2, count // 16, block), lambda j, core: (0, 0, 0, j)),
        ),
        out_shape=jax.ShapeDtypeStruct((16, 2, count // 16, hid), jnp.bfloat16),
        compiler_params=pltpu.CompilerParams(vmem_limit_bytes=32 * 1024 * 1024),
        cost_estimate=pl.CostEstimate(
            flops=8 * count * feat * hid, bytes_accessed=8 * feat * hid, transcendentals=0
        ),
        name="chip_terms",
    )(core, tokens, w_in, w_in_swap, w_out, w_out_swap)


def body(inputs, out_grad, w_in, w_out):
    bf16, f32 = jnp.bfloat16, jnp.float32
    feat, hid = w_in.shape
    rows = inputs.shape[0]
    part = rows // 2
    core = lax.axis_index("core")
    first = core == 0

    w_in_swap = lax.ppermute(w_in, "core", SWAP)
    w_out_swap = lax.ppermute(w_out, "core", SWAP)

    with jax.named_scope("gather_tokens"):
        own = jnp.stack([inputs, out_grad]).reshape(2, 2, part, feat).transpose(1, 0, 2, 3)
        own = jnp.broadcast_to(own[None], (8, 2, 2, part, feat)).reshape(16, 2, part, feat)
        by_y = lax.all_to_all(own, SIDE, 0, 0, tiled=True).reshape(8, 2, 2, part, feat)
        by_y = by_y.transpose(1, 2, 0, 3, 4).reshape(2, 2, 8 * part, feat)
        by_x = jnp.broadcast_to(by_y[None], (4,) + by_y.shape)
        by_x = lax.all_to_all(by_x, "x", 0, 0, tiled=True)
        near = lax.dynamic_index_in_dim(by_x, core, 1, False)
        far = lax.dynamic_index_in_dim(by_x, 1 - core, 1, False)

    with jax.named_scope("row_sum"):
        terms = chip_terms(core.reshape(1), by_x, w_in, w_in_swap, w_out, w_out_swap)
        terms = lax.all_to_all(terms, ROW, 0, 0, tiled=True)
        sums = terms.reshape(8, 2, 2, 2, part, hid).astype(f32).sum(axis=0)
        pre_act, back_grad = (
            sums[:, k].transpose(1, 0, 2, 3).reshape(2 * rows, hid) for k in (0, 1)
        )

    with jax.named_scope("swap_tokens"):
        swapped = lax.ppermute(far, "core", SWAP)

        def both_halves(near, far):
            near, far = near.reshape(32, part, feat), far.reshape(32, part, feat)
            halves = [jnp.where(first, near, far), jnp.where(first, far, near)]
            return jnp.stack(halves, axis=1).reshape(32 * rows, feat)

        all_in = both_halves(near[:, 0], swapped[:, 0])
        all_grad = both_halves(near[:, 1], swapped[:, 1])

    act_value, pullback = jax.vjp(gelu_tanh, pre_act)
    activation = act_value.astype(bf16)
    pre_grad = pullback(back_grad)[0].astype(bf16)
    pre_grad = lax.all_gather(pre_grad, ROW, axis=0, tiled=True)

    with jax.named_scope("token_sum"):
        terms = dot(pre_grad, w_in, ((1,), (1,)), bf16).reshape(32, rows, feat)
        terms, activation = lax.optimization_barrier((terms, activation))
        terms = lax.all_to_all(terms, PLANE, 0, 0, tiled=True)
        grad_inputs = terms.astype(f32).sum(axis=0).astype(bf16)

    activation = lax.all_gather(activation, ROW, axis=0, tiled=True)
    grad_w_in = dot(all_in, pre_grad, ((0,), (0,)), bf16)
    grad_w_out = dot(activation, all_grad, ((0,), (0,)), bf16)
    return (grad_inputs, grad_w_in, grad_w_out)


def solution(mesh):
    fine = Mesh(mesh.devices.reshape(2, 8, 2, 4, 4), ("y_hi", "z", "core", "x", "y_lo"))
    plane = ("y_hi", "x", "y_lo")
    token_block, up_block, down_block = P(plane, ROW), P(ROW, plane), P(plane, ROW)
    return jax.shard_map(
        body,
        mesh=fine,
        in_specs=(token_block, token_block, up_block, down_block),
        out_specs=(token_block, up_block, down_block),
        check_vma=False,
    )
```

time: 139 us -> 138 us (level); the launches traced: 138 us -> 136 us
  blocking collectives: 87.7 us -> 33.4 us
  waiting for transfers between devices: 20.2 us -> 50.4 us
  starting transfers between devices: 14.3 us -> 34.2 us
  matrix products: 9.9 us -> 5.38 us
  Pallas kernels: 0 us -> 4.24 us
  local copies, waits for them, and re-layouts: 2.89 us -> 5.52 us
    all_to_all x2 -> x0, blocking collectives: 53.2 us -> none  [the longest x1 33.4 us: body(): parts = lax.all_to_all(parts, ROW, 0, 0, tiled=True)]
    all_to_all x1 -> x3, waiting for transfers between devices: 18.3 us -> 50.4 us  [the longest x1 20.6 us: body(): by_x = lax.all_to_all(by_x, 'x', 0, 0, tiled=True)]
    all_to_all x1 -> x3, starting transfers between devices: 5.18 us -> 23.9 us  [the longest x1 10.2 us: body(): lax.all_to_all(own, SIDE, 0, 0, tiled=True).reshape(8, 2, 2, part, feat)]
    dot_general x7 -> x3, matrix products: 9.9 us -> 5.38 us  [dot(): lax.dot_general(left, right, (dims, ((), ())), preferred_element_type=jnp...]
    pallas_call x0 -> x1, Pallas kernels: none -> 4.24 us  [chip_terms(): pl.pallas_call(terms_kernel, grid_spec=pltpu.PrefetchScalarGridSpec(num_s...]
    ppermute x1 -> x3, waiting for transfers between devices: 1.87 us -> 0.01 us  [the longest x1 0.01 us: body(): w_in_swap = lax.ppermute(w_in, 'core', SWAP)]
    ppermute x1 -> x3, starting transfers between devices: 5.23 us -> 6.33 us  [the longest x1 2.19 us: body(): w_out_swap = lax.ppermute(w_out, 'core', SWAP)]
  transfers between devices with their start and end apart: 3 -> 7, of which waited for: 2 -> 3; matrix products, arithmetic and copies ran while one was open for 3% -> 6% of each run, Pallas kernels for 0% -> 0%
where the time goes in v2:
time: 138 us; the launch traced here: 136 us
  waiting for transfers between devices  50.4 us (37%)
  starting transfers between devices  34.2 us (25%)
  blocking collectives  33.4 us (24%)
  local copies, waits for them, and re-layouts  5.52 us (4%)
  matrix products  5.38 us (4%)
  Pallas kernels  4.24 us (3%)
  other arithmetic  2.01 us (1%)
    all_to_all x1, waiting for transfers between devices, body(): by_x = lax.all_to_all(by_x, 'x', 0, 0, tiled=True)  20.6 us
    all_to_all x1, waiting for transfers between devices, body(): terms = lax.all_to_all(terms, ROW, 0, 0, tiled=True)  19.6 us
    all_gather x1, blocking collectives, body(): pre_grad = lax.all_gather(pre_grad, ROW, axis=0, tiled=True)  16.8 us
    all_gather x1, blocking collectives, body(): activation = lax.all_gather(activation, ROW, axis=0, tiled=True)  16.6 us
    all_to_all x1, starting transfers between devices, body(): lax.all_to_all(own, SIDE, 0, 0, tiled=True).reshape(8, 2, 2, part, feat)  10.2 us
    all_to_all x1, waiting for transfers between devices, body(): lax.all_to_all(own, SIDE, 0, 0, tiled=True).reshape(8, 2, 2, part, feat)  10.2 us
    all_to_all x1, starting transfers between devices, body(): terms = lax.all_to_all(terms, ROW, 0, 0, tiled=True)  10.2 us
    dot_general x3, matrix products, dot(): lax.dot_general(left, right, (dims, ((), ())), preferred_element_type=jnp...  5.38 us
  transfers between devices with their start and end apart: 7, of which 3 were waited for; matrix products, arithmetic and copies ran while one was open for 6% of the time, Pallas kernels for 0%

profile of v2, /device:TPU:1, one launch (start us, length us, event | category | flops | bytes accessed | tf_op | source)
XLA Modules:
  0.0 136.0 jit_solution(984300325551657731)
XLA Ops:
  0.6 0.9 maximum_bitcast_fusion
  1.5 0.8 broadcast_in_dim.6
  2.3 10.2 %all-to-all-start = ((bf16[16,2,8,768]{3,2,1,0:T(8,128)(2,1)}), bf16[16,2,8,768]{3,2,1,0:T(8,128)(2,1)S(1)}, u32[]{:S(2)}, u32[]{:S(2)}) async-start(bf16[16,2,8,768]{3,2,1,0:T(8,128)(2,1)} %bitcast.4), calls=%async_computation | async-start | bytes 786432 | tf_op jit(solution)/shard_map/gather_tokens/all_to_all | solution.py:83
  12.5 2.1 %collective-permute-start = (bf16[768,768]{1,0:T(8,128)(2,1)}, bf16[768,768]{1,0:T(8,128)(2,1)}, u32[]{:S(2)}, u32[]{:S(2)}) collective-permute-start(bf16[768,768]{1,0:T(8,128)(2,1)} %w_in.1), channel_id=1, source_target_pairs={{0,16},{16,0},{1,17},{17,1},{2,18},{18,2},{3,19},{19,3},{4,20},{20... | collective-permute-start | bytes 3538952 | tf_op jit(solution)/shard_map/ppermute | solution.py:77
  14.6 2.2 %collective-permute-start.1 = (bf16[768,768]{1,0:T(8,128)(2,1)S(1)}, bf16[768,768]{1,0:T(8,128)(2,1)}, u32[]{:S(2)}, u32[]{:S(2)}) collective-permute-start(bf16[768,768]{1,0:T(8,128)(2,1)S(1)} %copy-done), channel_id=1, source_target_pairs={{0,16},{16,0},{1,17},{17,1},{2,18},{18,2},{3,19},{19,3},{4,20},{20... | collective-permute-start | bytes 3538952 | tf_op jit(solution)/shard_map/ppermute | solution.py:78
  16.8 10.2 %all-to-all-done = bf16[16,2,8,768]{3,2,1,0:T(8,128)(2,1)S(1)} async-done(((bf16[16,2,8,768]{3,2,1,0:T(8,128)(2,1)}), bf16[16,2,8,768]{3,2,1,0:T(8,128)(2,1)S(1)}, u32[]{:S(2)}, u32[]{:S(2)}) %all-to-all-start) | async-done | bytes 393248 | tf_op jit(solution)/shard_map/gather_tokens/all_to_all | solution.py:83
  27.1 1.3 broadcast_in_dim.15
  28.4 3.6 %all-to-all-start.1 = ((bf16[4,2,2,64,768]{4,3,2,1,0:T(8,128)(2,1)}), bf16[4,2,2,64,768]{4,3,2,1,0:T(8,128)(2,1)S(1)}, u32[]{:S(2)}, u32[]{:S(2)}) async-start(bf16[4,2,2,64,768]{4,3,2,1,0:T(8,128)(2,1)} %broadcast_in_dim.15), calls=%async_computation.1 | async-start | bytes 3145728 | tf_op jit(solution)/shard_map/gather_tokens/all_to_all | solution.py:86
  32.0 0.0 collective-permute-done.w_in_swap
  32.0 20.6 %all-to-all-done.1.tokens = bf16[4,2,2,64,768]{4,3,2,1,0:T(8,128)(2,1)S(1)} async-done(((bf16[4,2,2,64,768]{4,3,2,1,0:T(8,128)(2,1)}), bf16[4,2,2,64,768]{4,3,2,1,0:T(8,128)(2,1)S(1)}, u32[]{:S(2)}, u32[]{:S(2)}) %all-to-all-start.1) | async-done | bytes 1572896 | tf_op jit(solution)/shard_map/gather_tokens/all_to_all | solution.py:86
  52.6 1.3 copy-done.1
  53.9 4.2 %chip_terms.1 = bf16[16,2,16,768]{3,2,1,0:T(8,128)(2,1)} custom-call(s32[1]{0:T(128)} %bitcast.core, bf16[4,2,2,64,768]{4,3,2,1,0:T(8,128)(2,1)S(1)} %all-to-all-done.1.tokens, bf16[768,768]{1,0:T(8,128)(2,1)S(1)} %copy-done.1, bf16[768,768]{1,0:T(8,128)(2,1)} %collective-permute-done.w_in_swap, bf16[768,768]{1,0:T(8,128)(2,1)S(1)} %copy-done, ...), custom_call_target="tpu_custom_call" | custom-call | flops 1207959552 | bytes 4718592 | tf_op jit(solution)/shard_map/row_sum/chip_terms/pallas_call | solution.py:46
  58.1 10.2 %all-to-all-start.2 = ((bf16[16,2,16,768]{3,2,1,0:T(8,128)(2,1)}), bf16[16,2,16,768]{3,2,1,0:T(8,128)(2,1)S(1)}, u32[]{:S(2)}, u32[]{:S(2)}) async-start(bf16[16,2,16,768]{3,2,1,0:T(8,128)(2,1)} %chip_terms.1), calls=%async_computation.2 | async-start | bytes 1572864 | tf_op jit(solution)/shard_map/row_sum/all_to_all | solution.py:92
  68.3 1.0 dynamic-slice_bitcast_fusion.1
  69.3 2.0 %collective-permute-start.2 = (bf16[4,2,64,768]{3,2,1,0:T(8,128)(2,1)}, bf16[4,2,64,768]{3,2,1,0:T(8,128)(2,1)S(1)}, u32[]{:S(2)}, u32[]{:S(2)}) collective-permute-start(bf16[4,2,64,768]{3,2,1,0:T(8,128)(2,1)} %get-tuple-element.12), channel_id=1, source_target_pairs={{0,16},{16,0},{1,17},{17,1},{2,18},{18,2},{3,19},{19,3},{4,20},{20... | collective-permute-start | bytes 2359304 | tf_op jit(solution)/shard_map/swap_tokens/ppermute | solution.py:99
  71.3 19.6 %all-to-all-done.2 = bf16[16,2,16,768]{3,2,1,0:T(8,128)(2,1)S(1)} async-done(((bf16[16,2,16,768]{3,2,1,0:T(8,128)(2,1)}), bf16[16,2,16,768]{3,2,1,0:T(8,128)(2,1)S(1)}, u32[]{:S(2)}, u32[]{:S(2)}) %all-to-all-start.2) | async-done | bytes 786464 | tf_op jit(solution)/shard_map/row_sum/all_to_all | solution.py:92
  90.9 0.1 convert_reduce_fusion
  91.0 0.0 copy-start.2
  91.1 0.1 fusion.7
  91.2 16.8 %all_gather.6 = bf16[512,768]{1,0:T(8,128)(2,1)S(1)} all-gather(bf16[32,768]{1,0:T(8,128)(2,1)S(1)} %get-tuple-element.16), channel_id=1, replica_groups=mesh['y_hi'=2,'z'=8,'core'=2,'x'=4,'y_lo'=4] {'z','core'}, dimensions={0}, use_global_device_ids=true | all-gather | bytes 835584 | tf_op jit(solution)/shard_map/all_gather | solution.py:112
  108.0 1.7 %convolution_convert_fusion.2 = bf16[512,768]{1,0:T(8,128)(2,1)} fusion(bf16[512,768]{1,0:T(8,128)(2,1)S(1)} %all_gather.6, bf16[768,768]{1,0:T(8,128)(2,1)S(1)} %copy-done.2), kind=kOutput, calls=%fused_computation.3 | convolution fusion | flops 604372992 | bytes 2752512 | tf_op jit(solution)/shard_map/token_sum/dot_general | solution.py:20
  109.7 3.9 %all-to-all-start.3 = ((bf16[32,16,768]{2,1,0:T(8,128)(2,1)}), bf16[32,16,768]{2,1,0:T(8,128)(2,1)S(1)}, u32[]{:S(2)}, u32[]{:S(2)}) async-start(bf16[32,16,768]{2,1,0:T(8,128)(2,1)} %bitcast.15), calls=%async_computation.3 | async-start | bytes 1572864 | tf_op jit(solution)/shard_map/token_sum/all_to_all | solution.py:117
  113.6 0.0 collective-permute-done.2
  113.6 0.1 broadcast_select_fusion.1
  113.7 0.1 pad_maximum_fusion
  113.8 0.0 copy-start.4
  113.8 0.1 pad_maximum_fusion.1
  113.9 1.0 copy-done.4
  115.0 1.8 %convolution_convert_fusion.1 = bf16[768,768]{1,0:T(8,128)(2,1)} fusion(bf16[512,768]{1,0:T(8,128)(2,1)S(1)} %bitcast.80, bf16[512,768]{1,0:T(8,128)(2,1)S(1)} %copy-done.4), kind=kOutput, calls=%fused_computation.2 | convolution fusion | flops 604569600 | bytes 2752512 | tf_op jit(solution)/shard_map/dot_general | solution.py:20
  116.8 16.6 %all_gather.7 = bf16[512,768]{1,0:T(8,128)(2,1)S(1)} all-gather(bf16[32,768]{1,0:T(8,128)(2,1)S(1)} %get-tuple-element.6), channel_id=1, replica_groups=mesh['y_hi'=2,'z'=8,'core'=2,'x'=4,'y_lo'=4] {'z','core'}, dimensions={0}, use_global_device_ids=true | all-gather | bytes 835584 | tf_op jit(solution)/shard_map/all_gather | solution.py:120
  133.4 1.8 %convolution_convert_fusion = bf16[768,768]{1,0:T(8,128)(2,1)} fusion(bf16[512,768]{1,0:T(8,128)(2,1)S(1)} %all_gather.7, bf16[512,768]{1,0:T(8,128)(2,1)S(1)} %bitcast.81), kind=kOutput, calls=%fused_computation.1 | convolution fusion | flops 604569600 | bytes 2752512 | tf_op jit(solution)/shard_map/dot_general | solution.py:20
  135.2 0.7 reduce_sum.22
  (13 shorter events, 0.1 us)
Async XLA Ops:
  0.6 14.0 %copy-start = (bf16[768,768]{1,0:T(8,128)(2,1)S(1)}, bf16[768,768]{1,0:T(8,128)(2,1)}, u32[]{:S(2)}) copy-start(bf16[768,768]{1,0:T(8,128)(2,1)} %w_out.1) | copy-start | bytes 3538948
  2.3 24.8 %all-to-all-start = ((bf16[16,2,8,768]{3,2,1,0:T(8,128)(2,1)}), bf16[16,2,8,768]{3,2,1,0:T(8,128)(2,1)S(1)}, u32[]{:S(2)}, u32[]{:S(2)}) async-start(bf16[16,2,8,768]{3,2,1,0:T(8,128)(2,1)} %bitcast.4), calls=%async_computation | async-start | bytes 786432 | tf_op jit(solution)/shard_map/gather_tokens/all_to_all | solution.py:83
  12.5 19.5 %collective-permute-start = (bf16[768,768]{1,0:T(8,128)(2,1)}, bf16[768,768]{1,0:T(8,128)(2,1)}, u32[]{:S(2)}, u32[]{:S(2)}) collective-permute-start(bf16[768,768]{1,0:T(8,128)(2,1)} %w_in.1), channel_id=1, source_target_pairs={{0,16},{16,0},{1,17},{17,1},{2,18},{18,2},{3,19},{19,3},{4,20},{20... | collective-permute-start | bytes 3538952 | tf_op jit(solution)/shard_map/ppermute | solution.py:77
  14.6 17.4 %collective-permute-start.1 = (bf16[768,768]{1,0:T(8,128)(2,1)S(1)}, bf16[768,768]{1,0:T(8,128)(2,1)}, u32[]{:S(2)}, u32[]{:S(2)}) collective-permute-start(bf16[768,768]{1,0:T(8,128)(2,1)S(1)} %copy-done), channel_id=1, source_target_pairs={{0,16},{16,0},{1,17},{17,1},{2,18},{18,2},{3,19},{19,3},{4,20},{20... | collective-permute-start | bytes 3538952 | tf_op jit(solution)/shard_map/ppermute | solution.py:78
  28.4 24.2 %all-to-all-start.1 = ((bf16[4,2,2,64,768]{4,3,2,1,0:T(8,128)(2,1)}), bf16[4,2,2,64,768]{4,3,2,1,0:T(8,128)(2,1)S(1)}, u32[]{:S(2)}, u32[]{:S(2)}) async-start(bf16[4,2,2,64,768]{4,3,2,1,0:T(8,128)(2,1)} %broadcast_in_dim.15), calls=%async_computation.1 | async-start | bytes 3145728 | tf_op jit(solution)/shard_map/gather_tokens/all_to_all | solution.py:86
  52.6 1.3 copy-start.1
  58.1 32.8 %all-to-all-start.2 = ((bf16[16,2,16,768]{3,2,1,0:T(8,128)(2,1)}), bf16[16,2,16,768]{3,2,1,0:T(8,128)(2,1)S(1)}, u32[]{:S(2)}, u32[]{:S(2)}) async-start(bf16[16,2,16,768]{3,2,1,0:T(8,128)(2,1)} %chip_terms.1), calls=%async_computation.2 | async-start | bytes 1572864 | tf_op jit(solution)/shard_map/row_sum/all_to_all | solution.py:92
  69.3 44.3 %collective-permute-start.2 = (bf16[4,2,64,768]{3,2,1,0:T(8,128)(2,1)}, bf16[4,2,64,768]{3,2,1,0:T(8,128)(2,1)S(1)}, u32[]{:S(2)}, u32[]{:S(2)}) collective-permute-start(bf16[4,2,64,768]{3,2,1,0:T(8,128)(2,1)} %get-tuple-element.12), channel_id=1, source_target_pairs={{0,16},{16,0},{1,17},{17,1},{2,18},{18,2},{3,19},{19,3},{4,20},{20... | collective-permute-start | bytes 2359304 | tf_op jit(solution)/shard_map/swap_tokens/ppermute | solution.py:99
  91.0 16.9 %copy-start.2 = (bf16[768,768]{1,0:T(8,128)(2,1)S(1)}, bf16[768,768]{1,0:T(8,128)(2,1)}, u32[]{:S(2)}) copy-start(bf16[768,768]{1,0:T(8,128)(2,1)} %w_in.1) | copy-start | bytes 3538948
  108.0 1.7 %copy-start.3 = (bf16[512,768]{1,0:T(8,128)(2,1)}, bf16[512,768]{1,0:T(8,128)(2,1)S(1)}, u32[]{:S(2)}) copy-start(bf16[512,768]{1,0:T(8,128)(2,1)S(1)} %all_gather.6) | copy-start | bytes 2359300
  109.7 25.5 %all-to-all-start.3 = ((bf16[32,16,768]{2,1,0:T(8,128)(2,1)}), bf16[32,16,768]{2,1,0:T(8,128)(2,1)S(1)}, u32[]{:S(2)}, u32[]{:S(2)}) async-start(bf16[32,16,768]{2,1,0:T(8,128)(2,1)} %bitcast.15), calls=%async_computation.3 | async-start | bytes 1572864 | tf_op jit(solution)/shard_map/token_sum/all_to_all | solution.py:117
  113.8 1.1 copy-start.4

commit v3 on v2

v3 whole, which is shorter than its diff:
```python
import jax
import jax.numpy as jnp
from jax import lax
from jax.experimental import pallas as pl
from jax.experimental.pallas import tpu as pltpu
from jax.sharding import Mesh
from jax.sharding import PartitionSpec as P

PLANE = ("x", "y_hi", "y_lo")
SIDE = ("y_hi", "y_lo", "core")
ROW = ("z", "core")
SWAP = [(0, 1), (1, 0)]
ROW_ORDER = [[2 * z + core for z in range(7, -1, -1) for core in (0, 1)]]


def gelu_tanh(value):
    return jax.nn.gelu(value, approximate=True)


def dot(left, right, dims, out=jnp.float32):
    return lax.dot_general(
        left, right, (dims, ((), ())), preferred_element_type=jnp.float32
    ).astype(out)


def terms_kernel(core, tokens, w_in, w_in_swap, w_out, w_out_swap, terms, up, down, sems):
    near, far = core[0], 1 - core[0]
    blocks, _, feat, block = up.shape
    count = tokens.shape[0] * tokens.shape[3]

    def fetches(j):
        span = pl.ds(j * block, block)
        pairs = (
            (w_in.at[:, span], up.at[j, 0]),
            (w_in_swap.at[:, span], up.at[j, 1]),
            (w_out.at[span, :], down.at[j, 0]),
            (w_out_swap.at[span, :], down.at[j, 1]),
        )
        return [
            pltpu.make_async_copy(source, target, sems.at[j, k])
            for k, (source, target) in enumerate(pairs)
        ]

    for j in range(blocks):
        for fetch in fetches(j):
            fetch.start()

    def lhs(side, kind):
        return tokens[:, side, kind].reshape(count, feat)

    for j in range(blocks):
        for fetch in fetches(j):
            fetch.wait()
        pre = dot(lhs(near, 0), up[j, 0], ((1,), (0,)))
        pre += dot(lhs(far, 0), up[j, 1], ((1,), (0,)))
        back = dot(lhs(near, 1), down[j, 0], ((1,), (1,)))
        back += dot(lhs(far, 1), down[j, 1], ((1,), (1,)))
        for kind, value in enumerate((pre, back)):
            terms[:, kind, :, pl.ds(j * block, block)] = value.astype(terms.dtype).reshape(
                16, count // 16, block
            )


def chip_terms(core, tokens, *weights):
    feat, hid = weights[0].shape
    weights = [pltpu.with_memory_space_constraint(w, pltpu.HBM) for w in weights]
    block = 256
    blocks = hid // block
    count = tokens.shape[0] * tokens.shape[3]
    far = pl.BlockSpec(memory_space=pltpu.HBM)
    near = pl.BlockSpec(memory_space=pltpu.VMEM)
    return pl.pallas_call(
        terms_kernel,
        in_specs=[pl.BlockSpec(memory_space=pltpu.SMEM), near, far, far, far, far],
        out_specs=near,
        out_shape=jax.ShapeDtypeStruct((16, 2, count // 16, hid), jnp.bfloat16),
        scratch_shapes=[
            pltpu.VMEM((blocks, 2, feat, block), jnp.bfloat16),
            pltpu.VMEM((blocks, 2, block, feat), jnp.bfloat16),
            pltpu.SemaphoreType.DMA((blocks, 4)),
        ],
        compiler_params=pltpu.CompilerParams(vmem_limit_bytes=32 * 1024 * 1024),
        cost_estimate=pl.CostEstimate(
            flops=8 * count * feat * hid, bytes_accessed=8 * feat * hid, transcendentals=0
        ),
        name="chip_terms",
    )(core, tokens, *weights)


def body(inputs, out_grad, w_in, w_out):
    bf16, f32 = jnp.bfloat16, jnp.float32
    feat, hid = w_in.shape
    rows = inputs.shape[0]
    part = rows // 2
    core = lax.axis_index("core")
    first = core == 0

    with jax.named_scope("gather_tokens"):
        halves = [x.reshape(2, part, feat) for x in (inputs, out_grad)]
        own = jnp.concatenate(halves, axis=1)[None]
        own = jnp.broadcast_to(own, (8, 2, rows, feat)).reshape(16, rows, feat)
        by_y = lax.all_to_all(own, SIDE, 0, 0, tiled=True)
        by_y, w_in_own, w_out_own = lax.optimization_barrier((by_y, w_in, w_out))
        by_y = by_y.reshape(8, 2, 2, part, feat)
        by_y = by_y.transpose(1, 2, 0, 3, 4).reshape(2, 2, 8 * part, feat)
        by_x = jnp.broadcast_to(by_y[None], (4,) + by_y.shape)
        by_x = lax.all_to_all(by_x, "x", 0, 0, tiled=True)
        w_in_swap = lax.ppermute(w_in_own, "core", SWAP)
        w_out_swap = lax.ppermute(w_out_own, "core", SWAP)
        near = lax.dynamic_index_in_dim(by_x, core, 1, False)
        far = lax.dynamic_index_in_dim(by_x, 1 - core, 1, False)

    with jax.named_scope("row_sum"):
        terms = chip_terms(core.reshape(1), by_x, w_in, w_in_swap, w_out, w_out_swap)
        terms = lax.all_to_all(terms, ROW, 0, 0, axis_index_groups=ROW_ORDER, tiled=True)

    with jax.named_scope("swap_tokens"):
        swapped = lax.ppermute(far, "core", SWAP)

        def both_halves(near, far):
            near, far = near.reshape(32, part, feat), far.reshape(32, part, feat)
            halves = [jnp.where(first, near, far), jnp.where(first, far, near)]
            return jnp.stack(halves, axis=1).reshape(32 * rows, feat)

        all_in = both_halves(near[:, 0], swapped[:, 0])
        all_grad = both_halves(near[:, 1], swapped[:, 1])

    sums, all_in, all_grad = lax.optimization_barrier((terms, all_in, all_grad))
    sums = sums.reshape(8, 2, 2, 2, part, hid).astype(f32).sum(axis=0)
    pre_act, back_grad = (
        sums[:, k].transpose(1, 0, 2, 3).reshape(2 * rows, hid) for k in (0, 1)
    )
    act_value, pullback = jax.vjp(gelu_tanh, pre_act)
    activation = act_value.astype(bf16)
    pre_grad = pullback(back_grad)[0].astype(bf16)
    pre_grad = lax.all_gather(pre_grad, ROW, axis_index_groups=ROW_ORDER, axis=0, tiled=True)

    with jax.named_scope("token_sum"):
        terms = dot(pre_grad, w_in, ((1,), (1,)), bf16).reshape(32, rows, feat)
        terms, activation = lax.optimization_barrier((terms, activation))
        terms = lax.all_to_all(terms, PLANE, 0, 0, tiled=True)
        grad_inputs = terms.astype(f32).sum(axis=0).astype(bf16)

    activation = lax.all_gather(activation, ROW, axis_index_groups=ROW_ORDER, axis=0, tiled=True)
    activation, pre_grad = lax.optimization_barrier((activation, pre_grad))
    grad_w_in = dot(all_in, pre_grad, ((0,), (0,)), bf16)
    grad_w_out = dot(activation, all_grad, ((0,), (0,)), bf16)
    return (grad_inputs, grad_w_in, grad_w_out)


def solution(mesh):
    fine = Mesh(mesh.devices.reshape(2, 8, 2, 4, 4), ("y_hi", "z", "core", "x", "y_lo"))
    plane = ("y_hi", "x", "y_lo")
    token_block, up_block, down_block = P(plane, ROW), P(ROW, plane), P(plane, ROW)
    return jax.shard_map(
        body,
        mesh=fine,
        in_specs=(token_block, token_block, up_block, down_block),
        out_specs=(token_block, up_block, down_block),
        check_vma=False,
    )
```

time: 138 us -> 134 us (0.971)
  blocking collectives: 33.4 us -> 60.2 us
  waiting for transfers between devices: 50.4 us -> 31.5 us
  starting transfers between devices: 34.2 us -> 26.9 us
  local copies, waits for them, and re-layouts: 5.52 us -> 2.42 us
    all_to_all x0 -> x1, blocking collectives: none -> 23.9 us  [body(): by_y = lax.all_to_all(own, SIDE, 0, 0, tiled=True)]
    all_to_all x2 -> x1, waiting for transfers between devices: 29.8 us -> 13.1 us  [body(): lax.all_to_all(terms, ROW, 0, 0, axis_index_groups=ROW_ORDER, tiled=True)]
    all_to_all x2 -> x1, starting transfers between devices: 20.4 us -> 12.7 us  [body(): lax.all_to_all(terms, ROW, 0, 0, axis_index_groups=ROW_ORDER, tiled=True)]
    all_to_all x1, waiting for transfers between devices: 20.6 us -> 16.3 us  [body(): by_x = lax.all_to_all(by_x, 'x', 0, 0, tiled=True)]
    all_gather x2, blocking collectives: 33.4 us -> 36.4 us  [the longest x1 18.8 us: body(): lax.all_gather(activation, ROW, axis_index_groups=ROW_ORDER, axis=0, tile...]
    unnamed x10 -> x4, local copies, waits for them, and re-layouts: 2.33 us -> 0.01 us
    ppermute x1, waiting for transfers between devices: 0.01 us -> 2.11 us  [body(): swapped = lax.ppermute(far, 'core', SWAP)]
  transfers between devices with their start and end apart: 7 -> 6, of which waited for: 3 -> 3; matrix products, arithmetic and copies ran while one was open for 6% -> 4% of each run, Pallas kernels for 0% -> 0%
where the time goes in v3:
time: 134 us; the launch traced here: 133 us
  blocking collectives  60.2 us (45%)
  waiting for transfers between devices  31.5 us (24%)
  starting transfers between devices  26.9 us (20%)
  matrix products  5.34 us (4%)
  Pallas kernels  4.13 us (3%)
  local copies, waits for them, and re-layouts  2.42 us (2%)
  other arithmetic  1.91 us (1%)
    all_to_all x1, blocking collectives, body(): by_y = lax.all_to_all(own, SIDE, 0, 0, tiled=True)  23.9 us
    all_gather x1, blocking collectives, body(): lax.all_gather(activation, ROW, axis_index_groups=ROW_ORDER, axis=0, tile...  18.8 us
    all_gather x1, blocking collectives, body(): lax.all_gather(pre_grad, ROW, axis_index_groups=ROW_ORDER, axis=0, tiled=...  17.6 us
    all_to_all x1, waiting for transfers between devices, body(): by_x = lax.all_to_all(by_x, 'x', 0, 0, tiled=True)  16.3 us
    all_to_all x1, waiting for transfers between devices, body(): lax.all_to_all(terms, ROW, 0, 0, axis_index_groups=ROW_ORDER, tiled=True)  13.1 us
    all_to_all x1, starting transfers between devices, body(): lax.all_to_all(terms, ROW, 0, 0, axis_index_groups=ROW_ORDER, tiled=True)  12.7 us
    dot_general x3, matrix products, dot(): lax.dot_general(left, right, (dims, ((), ())), preferred_element_type=jnp...  5.34 us
    pallas_call x1, Pallas kernels, chip_terms(): pl.pallas_call(terms_kernel, in_specs=[pl.BlockSpec(memory_space=pltpu.SM...  4.13 us
  transfers between devices with their start and end apart: 6, of which 3 were waited for; matrix products, arithmetic and copies ran while one was open for 4% of the time, Pallas kernels for 0%

profile of v3, /device:TPU:1, one launch (start us, length us, event | category | flops | bytes accessed | tf_op | source)
XLA Modules:
  0.0 133.2 jit_solution(14798881855892062043)
XLA Ops:
  0.6 0.8 pad_maximum_fusion.2
  1.4 23.9 %all_to_all.20 = bf16[16,16,768]{2,1,0:T(8,128)(2,1)S(1)} all-to-all(bf16[16,16,768]{2,1,0:T(8,128)(2,1)S(1)} %bitcast.72), channel_id=1, replica_groups=mesh['y_hi'=2,'z'=8,'core'=2,'x'=4,'y_lo'=4] {'y_hi','y_lo','core'}, dimensions={0} | all-to-all | bytes 786432 | tf_op jit(solution)/shard_map/gather_tokens/all_to_all | solution.py:102
  25.3 1.3 broadcast_in_dim.15
  26.6 0.0 copy-start
  26.6 3.7 %all-to-all-start.1 = ((bf16[4,2,2,64,768]{4,3,2,1,0:T(8,128)(2,1)}), bf16[4,2,2,64,768]{4,3,2,1,0:T(8,128)(2,1)S(1)}, u32[]{:S(2)}, u32[]{:S(2)}) async-start(bf16[4,2,2,64,768]{4,3,2,1,0:T(8,128)(2,1)} %broadcast_in_dim.15), calls=%async_computation.1 | async-start | bytes 3145728 | tf_op jit(solution)/shard_map/gather_tokens/all_to_all | solution.py:107
  30.3 1.9 %collective-permute-start = (bf16[768,768]{1,0:T(8,128)(2,1)}, bf16[768,768]{1,0:T(8,128)(2,1)}, u32[]{:S(2)}, u32[]{:S(2)}) collective-permute-start(bf16[768,768]{1,0:T(8,128)(2,1)} %w_in.1), channel_id=1, source_target_pairs={{0,16},{16,0},{1,17},{17,1},{2,18},{18,2},{3,19},{19,3},{4,20},{20... | collective-permute-start | bytes 3538952 | tf_op jit(solution)/shard_map/gather_tokens/ppermute | solution.py:108
  32.3 0.0 copy-done
  32.3 2.4 %collective-permute-start.1 = (bf16[768,768]{1,0:T(8,128)(2,1)S(1)}, bf16[768,768]{1,0:T(8,128)(2,1)}, u32[]{:S(2)}, u32[]{:S(2)}) collective-permute-start(bf16[768,768]{1,0:T(8,128)(2,1)S(1)} %copy-done), channel_id=1, source_target_pairs={{0,16},{16,0},{1,17},{17,1},{2,18},{18,2},{3,19},{19,3},{4,20},{20... | collective-permute-start | bytes 3538952 | tf_op jit(solution)/shard_map/gather_tokens/ppermute | solution.py:109
  34.7 16.3 %all-to-all-done.1.tokens = bf16[4,2,2,64,768]{4,3,2,1,0:T(8,128)(2,1)S(1)} async-done(((bf16[4,2,2,64,768]{4,3,2,1,0:T(8,128)(2,1)}), bf16[4,2,2,64,768]{4,3,2,1,0:T(8,128)(2,1)S(1)}, u32[]{:S(2)}, u32[]{:S(2)}) %all-to-all-start.1) | async-done | bytes 1572896 | tf_op jit(solution)/shard_map/gather_tokens/all_to_all | solution.py:107
  50.9 0.0 collective-permute-done.w_in_swap
  50.9 0.0 collective-permute-done.1.w_out_swap
  50.9 4.1 %chip_terms.1 = bf16[16,2,16,768]{3,2,1,0:T(8,128)(2,1)} custom-call(s32[1]{0:T(128)} %bitcast.core, bf16[4,2,2,64,768]{4,3,2,1,0:T(8,128)(2,1)S(1)} %all-to-all-done.1.tokens, bf16[768,768]{1,0:T(8,128)(2,1)} %w_in.1, bf16[768,768]{1,0:T(8,128)(2,1)} %collective-permute-done.w_in_swap, bf16[768,768]{1,0:T(8,128)(2,1)} %w_out.1, ...), custom_call_target="tpu_custom_call" | custom-call | flops 1207959552 | bytes 4718592 | tf_op jit(solution)/shard_map/row_sum/chip_terms/pallas_call | solution.py:72
  55.1 12.7 %all-to-all-start.2 = ((bf16[16,2,16,768]{3,2,1,0:T(8,128)(2,1)}), bf16[16,2,16,768]{3,2,1,0:T(8,128)(2,1)S(1)}, u32[]{:S(2)}, u32[]{:S(2)}) async-start(bf16[16,2,16,768]{3,2,1,0:T(8,128)(2,1)} %chip_terms.1), calls=%async_computation.2 | async-start | bytes 1572864 | tf_op jit(solution)/shard_map/row_sum/all_to_all | solution.py:115
  67.8 1.0 dynamic-slice_bitcast_fusion.1
  68.8 2.3 %collective-permute-start.2 = (bf16[4,2,64,768]{3,2,1,0:T(8,128)(2,1)}, bf16[4,2,64,768]{3,2,1,0:T(8,128)(2,1)S(1)}, u32[]{:S(2)}, u32[]{:S(2)}) collective-permute-start(bf16[4,2,64,768]{3,2,1,0:T(8,128)(2,1)} %get-tuple-element.28), channel_id=1, source_target_pairs={{0,16},{16,0},{1,17},{17,1},{2,18},{18,2},{3,19},{19,3},{4,20},{20... | collective-permute-start | bytes 2359304 | tf_op jit(solution)/shard_map/swap_tokens/ppermute | solution.py:118
  71.1 2.1 %collective-permute-done.2 = bf16[4,2,64,768]{3,2,1,0:T(8,128)(2,1)S(1)} collective-permute-done((bf16[4,2,64,768]{3,2,1,0:T(8,128)(2,1)}, bf16[4,2,64,768]{3,2,1,0:T(8,128)(2,1)S(1)}, u32[]{:S(2)}, u32[]{:S(2)}) %collective-permute-start.2) | collective-permute-done | bytes 786464 | tf_op jit(solution)/shard_map/swap_tokens/ppermute | solution.py:118
  73.2 0.1 broadcast_select_fusion.1
  73.3 0.1 pad_maximum_fusion
  73.4 0.1 pad_maximum_fusion.1
  73.5 13.1 %all-to-all-done.2 = bf16[16,2,16,768]{3,2,1,0:T(8,128)(2,1)S(1)} async-done(((bf16[16,2,16,768]{3,2,1,0:T(8,128)(2,1)}), bf16[16,2,16,768]{3,2,1,0:T(8,128)(2,1)S(1)}, u32[]{:S(2)}, u32[]{:S(2)}) %all-to-all-start.2) | async-done | bytes 786464 | tf_op jit(solution)/shard_map/row_sum/all_to_all | solution.py:115
  86.6 0.1 convert_reduce_fusion
  86.7 0.0 copy-start.1
  86.8 0.1 fusion.7
  86.8 17.6 %all_gather.6 = bf16[512,768]{1,0:T(8,128)(2,1)S(1)} all-gather(bf16[32,768]{1,0:T(8,128)(2,1)S(1)} %get-tuple-element.32), channel_id=1, replica_groups={{224,240,192,208,160,176,128,144,96,112,64,80,32,48,0,16},{225,241,193,..., dimensions={0}, use_global_device_ids=true | all-gather | bytes 835584 | tf_op jit(solution)/shard_map/all_gather | solution.py:136
  104.4 0.0 copy-done.1
  104.4 1.7 %convolution_convert_fusion.2 = bf16[512,768]{1,0:T(8,128)(2,1)} fusion(bf16[512,768]{1,0:T(8,128)(2,1)S(1)} %all_gather.6, bf16[768,768]{1,0:T(8,128)(2,1)S(1)} %copy-done.1), kind=kOutput, calls=%fused_computation.3 | convolution fusion | flops 604372992 | bytes 2752512 | tf_op jit(solution)/shard_map/token_sum/dot_general | solution.py:21
  106.1 3.9 %all-to-all-start.3 = ((bf16[32,16,768]{2,1,0:T(8,128)(2,1)}), bf16[32,16,768]{2,1,0:T(8,128)(2,1)S(1)}, u32[]{:S(2)}, u32[]{:S(2)}) async-start(bf16[32,16,768]{2,1,0:T(8,128)(2,1)} %bitcast.26), calls=%async_computation.3 | async-start | bytes 1572864 | tf_op jit(solution)/shard_map/token_sum/all_to_all | solution.py:141
  110.0 18.8 %all_gather.7 = bf16[512,768]{1,0:T(8,128)(2,1)S(1)} all-gather(bf16[32,768]{1,0:T(8,128)(2,1)S(1)} %get-tuple-element.19), channel_id=1, replica_groups={{224,240,192,208,160,176,128,144,96,112,64,80,32,48,0,16},{225,241,193,..., dimensions={0}, use_global_device_ids=true | all-gather | bytes 835584 | tf_op jit(solution)/shard_map/all_gather | solution.py:144
  128.9 1.8 %convolution_convert_fusion.1 = bf16[768,768]{1,0:T(8,128)(2,1)} fusion(bf16[512,768]{1,0:T(8,128)(2,1)S(1)} %bitcast.79, bf16[512,768]{1,0:T(8,128)(2,1)S(1)} %all_gather.6), kind=kOutput, calls=%fused_computation.2 | convolution fusion | flops 604569600 | bytes 2752512 | tf_op jit(solution)/shard_map/dot_general | solution.py:21
  130.7 1.8 %convolution_convert_fusion = bf16[768,768]{1,0:T(8,128)(2,1)} fusion(bf16[512,768]{1,0:T(8,128)(2,1)S(1)} %all_gather.7, bf16[512,768]{1,0:T(8,128)(2,1)S(1)} %bitcast.80), kind=kOutput, calls=%fused_computation.1 | convolution fusion | flops 604569600 | bytes 2752512 | tf_op jit(solution)/shard_map/dot_general | solution.py:21
  132.5 0.0 all-to-all-done.3
  132.5 0.7 reduce_sum.22
  (5 shorter events, 0.1 us)
Async XLA Ops:
  26.6 5.6 %copy-start = (bf16[768,768]{1,0:T(8,128)(2,1)S(1)}, bf16[768,768]{1,0:T(8,128)(2,1)}, u32[]{:S(2)}) copy-start(bf16[768,768]{1,0:T(8,128)(2,1)} %w_out.1) | copy-start | bytes 3538948
  26.6 24.3 %all-to-all-start.1 = ((bf16[4,2,2,64,768]{4,3,2,1,0:T(8,128)(2,1)}), bf16[4,2,2,64,768]{4,3,2,1,0:T(8,128)(2,1)S(1)}, u32[]{:S(2)}, u32[]{:S(2)}) async-start(bf16[4,2,2,64,768]{4,3,2,1,0:T(8,128)(2,1)} %broadcast_in_dim.15), calls=%async_computation.1 | async-start | bytes 3145728 | tf_op jit(solution)/shard_map/gather_tokens/all_to_all | solution.py:107
  30.3 20.6 %collective-permute-start = (bf16[768,768]{1,0:T(8,128)(2,1)}, bf16[768,768]{1,0:T(8,128)(2,1)}, u32[]{:S(2)}, u32[]{:S(2)}) collective-permute-start(bf16[768,768]{1,0:T(8,128)(2,1)} %w_in.1), channel_id=1, source_target_pairs={{0,16},{16,0},{1,17},{17,1},{2,18},{18,2},{3,19},{19,3},{4,20},{20... | collective-permute-start | bytes 3538952 | tf_op jit(solution)/shard_map/gather_tokens/ppermute | solution.py:108
  32.3 18.7 %collective-permute-start.1 = (bf16[768,768]{1,0:T(8,128)(2,1)S(1)}, bf16[768,768]{1,0:T(8,128)(2,1)}, u32[]{:S(2)}, u32[]{:S(2)}) collective-permute-start(bf16[768,768]{1,0:T(8,128)(2,1)S(1)} %copy-done), channel_id=1, source_target_pairs={{0,16},{16,0},{1,17},{17,1},{2,18},{18,2},{3,19},{19,3},{4,20},{20... | collective-permute-start | bytes 3538952 | tf_op jit(solution)/shard_map/gather_tokens/ppermute | solution.py:109
  55.1 31.5 %all-to-all-start.2 = ((bf16[16,2,16,768]{3,2,1,0:T(8,128)(2,1)}), bf16[16,2,16,768]{3,2,1,0:T(8,128)(2,1)S(1)}, u32[]{:S(2)}, u32[]{:S(2)}) async-start(bf16[16,2,16,768]{3,2,1,0:T(8,128)(2,1)} %chip_terms.1), calls=%async_computation.2 | async-start | bytes 1572864 | tf_op jit(solution)/shard_map/row_sum/all_to_all | solution.py:115
  68.8 4.4 %collective-permute-start.2 = (bf16[4,2,64,768]{3,2,1,0:T(8,128)(2,1)}, bf16[4,2,64,768]{3,2,1,0:T(8,128)(2,1)S(1)}, u32[]{:S(2)}, u32[]{:S(2)}) collective-permute-start(bf16[4,2,64,768]{3,2,1,0:T(8,128)(2,1)} %get-tuple-element.28), channel_id=1, source_target_pairs={{0,16},{16,0},{1,17},{17,1},{2,18},{18,2},{3,19},{19,3},{4,20},{20... | collective-permute-start | bytes 2359304 | tf_op jit(solution)/shard_map/swap_tokens/ppermute | solution.py:118
  86.7 17.7 %copy-start.1 = (bf16[768,768]{1,0:T(8,128)(2,1)S(1)}, bf16[768,768]{1,0:T(8,128)(2,1)}, u32[]{:S(2)}) copy-start(bf16[768,768]{1,0:T(8,128)(2,1)} %w_in.1) | copy-start | bytes 3538948
  106.1 26.4 %all-to-all-start.3 = ((bf16[32,16,768]{2,1,0:T(8,128)(2,1)}), bf16[32,16,768]{2,1,0:T(8,128)(2,1)S(1)}, u32[]{:S(2)}, u32[]{:S(2)}) async-start(bf16[32,16,768]{2,1,0:T(8,128)(2,1)} %bitcast.26), calls=%async_computation.3 | async-start | bytes 1572864 | tf_op jit(solution)/shard_map/token_sum/all_to_all | solution.py:141

commit v4 on v3

--- a/solution.py
+++ b/solution.py
@@ -10,6 +10,8 @@
 SIDE = ("y_hi", "y_lo", "core")
 ROW = ("z", "core")
 SWAP = [(0, 1), (1, 0)]
+SIDE_ORDER = [[2 * y + core for y in range(7, -1, -1) for core in (0, 1)]]
+PLANE_ORDER = [[8 * x + y for x in range(3, -1, -1) for y in range(7, -1, -1)]]
 ROW_ORDER = [[2 * z + core for z in range(7, -1, -1) for core in (0, 1)]]
 
 
@@ -99,12 +101,14 @@
         halves = [x.reshape(2, part, feat) for x in (inputs, out_grad)]
         own = jnp.concatenate(halves, axis=1)[None]
         own = jnp.broadcast_to(own, (8, 2, rows, feat)).reshape(16, rows, feat)
-        by_y = lax.all_to_all(own, SIDE, 0, 0, tiled=True)
+        by_y = lax.all_to_all(own, SIDE, 0, 0, axis_index_groups=SIDE_ORDER, tiled=True)
         by_y, w_in_own, w_out_own = lax.optimization_barrier((by_y, w_in, w_out))
         by_y = by_y.reshape(8, 2, 2, part, feat)
         by_y = by_y.transpose(1, 2, 0, 3, 4).reshape(2, 2, 8 * part, feat)
         by_x = jnp.broadcast_to(by_y[None], (4,) + by_y.shape)
-        by_x = lax.all_to_all(by_x, "x", 0, 0, tiled=True)
+        by_x = lax.all_to_all(
+            by_x, "x", 0, 0, axis_index_groups=[[3, 2, 1, 0]], tiled=True
+        )
         w_in_swap = lax.ppermute(w_in_own, "core", SWAP)
         w_out_swap = lax.ppermute(w_out_own, "core", SWAP)
         near = lax.dynamic_index_in_dim(by_x, core, 1, False)
@@ -138,7 +142,9 @@
     with jax.named_scope("token_sum"):
         terms = dot(pre_grad, w_in, ((1,), (1,)), bf16).reshape(32, rows, feat)
         terms, activation = lax.optimization_barrier((terms, activation))
-        terms = lax.all_to_all(terms, PLANE, 0, 0, tiled=True)
+        terms = lax.all_to_all(
+            terms, PLANE, 0, 0, axis_index_groups=PLANE_ORDER, tiled=True
+        )
         grad_inputs = terms.astype(f32).sum(axis=0).astype(bf16)
 
     activation = lax.all_gather(activation, ROW, axis_index_groups=ROW_ORDER, axis=0, tiled=True)

time: 134 us -> 136 us (1.015)
  starting transfers between devices: 26.9 us -> 32.2 us
  blocking collectives: 60.2 us -> 58.4 us
  waiting for transfers between devices: 31.5 us -> 29.7 us
    all_to_all x2, starting transfers between devices: 7.6 us -> 12.6 us  [the longest x1 8.51 us: body(): lax.all_to_all(terms, PLANE, 0, 0, axis_index_groups=PLANE_ORDER, tiled=T...]
    all_to_all x1, blocking collectives: 23.9 us -> 21.6 us  [body(): lax.all_to_all(own, SIDE, 0, 0, axis_index_groups=SIDE_ORDER, tiled=True)]
    all_to_all x2, waiting for transfers between devices: 16.3 us -> 14.5 us  [the longest x1 14.5 us: body(): lax.all_to_all(by_x, 'x', 0, 0, axis_index_groups=[[3, 2, 1, 0]], tiled=T...]
where the time goes in v4:
time: 136 us; the launch traced here: 135 us
  blocking collectives  58.4 us (43%)
  starting transfers between devices  32.2 us (24%)
  waiting for transfers between devices  29.7 us (22%)
  matrix products  5.34 us (4%)
  Pallas kernels  4.13 us (3%)
  local copies, waits for them, and re-layouts  2.42 us (2%)
  other arithmetic  1.91 us (1%)
    all_to_all x1, blocking collectives, body(): lax.all_to_all(own, SIDE, 0, 0, axis_index_groups=SIDE_ORDER, tiled=True)  21.6 us
    all_gather x1, blocking collectives, body(): lax.all_gather(activation, ROW, axis_index_groups=ROW_ORDER, axis=0, tile...  19.3 us
    all_gather x1, blocking collectives, body(): lax.all_gather(pre_grad, ROW, axis_index_groups=ROW_ORDER, axis=0, tiled=...  17.6 us
    all_to_all x1, waiting for transfers between devices, body(): lax.all_to_all(by_x, 'x', 0, 0, axis_index_groups=[[3, 2, 1, 0]], tiled=T...  14.5 us
    all_to_all x1, waiting for transfers between devices, body(): lax.all_to_all(terms, ROW, 0, 0, axis_index_groups=ROW_ORDER, tiled=True)  13.1 us
    all_to_all x1, starting transfers between devices, body(): lax.all_to_all(terms, ROW, 0, 0, axis_index_groups=ROW_ORDER, tiled=True)  13.1 us
    all_to_all x1, starting transfers between devices, body(): lax.all_to_all(terms, PLANE, 0, 0, axis_index_groups=PLANE_ORDER, tiled=T...  8.51 us
    dot_general x3, matrix products, dot(): lax.dot_general(left, right, (dims, ((), ())), preferred_element_type=jnp...  5.34 us
  transfers between devices with their start and end apart: 6, of which 3 were waited for; matrix products, arithmetic and copies ran while one was open for 4% of the time, Pallas kernels for 0%

profile of v4, /device:TPU:1, one launch (start us, length us, event | category | flops | bytes accessed | tf_op | source)
XLA Modules:
  0.0 135.0 jit_solution(7819871301690024647)
XLA Ops:
  0.6 0.8 pad_maximum_fusion.2
  1.4 21.6 %all_to_all.20 = bf16[16,16,768]{2,1,0:T(8,128)(2,1)S(1)} all-to-all(bf16[16,16,768]{2,1,0:T(8,128)(2,1)S(1)} %bitcast.72), channel_id=1, replica_groups={{259,275,258,274,257,273,256,272,3,19,2,18,1,17,0,16},{263,279,262,278,..., dimensions={0} | all-to-all | bytes 786432 | tf_op jit(solution)/shard_map/gather_tokens/all_to_all | solution.py:104
  23.1 1.3 broadcast_in_dim.15
  24.4 0.0 copy-start
  24.4 4.1 %all-to-all-start.1 = ((bf16[4,2,2,64,768]{4,3,2,1,0:T(8,128)(2,1)}), bf16[4,2,2,64,768]{4,3,2,1,0:T(8,128)(2,1)S(1)}, u32[]{:S(2)}, u32[]{:S(2)}) async-start(bf16[4,2,2,64,768]{4,3,2,1,0:T(8,128)(2,1)} %broadcast_in_dim.15), calls=%async_computation.1 | async-start | bytes 3145728 | tf_op jit(solution)/shard_map/gather_tokens/all_to_all | solution.py:109
  28.5 2.4 %collective-permute-start = (bf16[768,768]{1,0:T(8,128)(2,1)}, bf16[768,768]{1,0:T(8,128)(2,1)}, u32[]{:S(2)}, u32[]{:S(2)}) collective-permute-start(bf16[768,768]{1,0:T(8,128)(2,1)} %w_in.1), channel_id=1, source_target_pairs={{0,16},{16,0},{1,17},{17,1},{2,18},{18,2},{3,19},{19,3},{4,20},{20... | collective-permute-start | bytes 3538952 | tf_op jit(solution)/shard_map/gather_tokens/ppermute | solution.py:112
  30.9 0.0 copy-done
  30.9 1.9 %collective-permute-start.1 = (bf16[768,768]{1,0:T(8,128)(2,1)S(1)}, bf16[768,768]{1,0:T(8,128)(2,1)}, u32[]{:S(2)}, u32[]{:S(2)}) collective-permute-start(bf16[768,768]{1,0:T(8,128)(2,1)S(1)} %copy-done), channel_id=1, source_target_pairs={{0,16},{16,0},{1,17},{17,1},{2,18},{18,2},{3,19},{19,3},{4,20},{20... | collective-permute-start | bytes 3538952 | tf_op jit(solution)/shard_map/gather_tokens/ppermute | solution.py:113
  32.8 14.5 %all-to-all-done.1.tokens = bf16[4,2,2,64,768]{4,3,2,1,0:T(8,128)(2,1)S(1)} async-done(((bf16[4,2,2,64,768]{4,3,2,1,0:T(8,128)(2,1)}), bf16[4,2,2,64,768]{4,3,2,1,0:T(8,128)(2,1)S(1)}, u32[]{:S(2)}, u32[]{:S(2)}) %all-to-all-start.1) | async-done | bytes 1572896 | tf_op jit(solution)/shard_map/gather_tokens/all_to_all | solution.py:109
  47.3 0.0 collective-permute-done.w_in_swap
  47.3 0.0 collective-permute-done.1.w_out_swap
  47.3 4.1 %chip_terms.1 = bf16[16,2,16,768]{3,2,1,0:T(8,128)(2,1)} custom-call(s32[1]{0:T(128)} %bitcast.core, bf16[4,2,2,64,768]{4,3,2,1,0:T(8,128)(2,1)S(1)} %all-to-all-done.1.tokens, bf16[768,768]{1,0:T(8,128)(2,1)} %w_in.1, bf16[768,768]{1,0:T(8,128)(2,1)} %collective-permute-done.w_in_swap, bf16[768,768]{1,0:T(8,128)(2,1)} %w_out.1, ...), custom_call_target="tpu_custom_call" | custom-call | flops 1207959552 | bytes 4718592 | tf_op jit(solution)/shard_map/row_sum/chip_terms/pallas_call | solution.py:74
  51.4 13.1 %all-to-all-start.2 = ((bf16[16,2,16,768]{3,2,1,0:T(8,128)(2,1)}), bf16[16,2,16,768]{3,2,1,0:T(8,128)(2,1)S(1)}, u32[]{:S(2)}, u32[]{:S(2)}) async-start(bf16[16,2,16,768]{3,2,1,0:T(8,128)(2,1)} %chip_terms.1), calls=%async_computation.2 | async-start | bytes 1572864 | tf_op jit(solution)/shard_map/row_sum/all_to_all | solution.py:119
  64.5 1.0 dynamic-slice_bitcast_fusion.1
  65.5 2.3 %collective-permute-start.2 = (bf16[4,2,64,768]{3,2,1,0:T(8,128)(2,1)}, bf16[4,2,64,768]{3,2,1,0:T(8,128)(2,1)S(1)}, u32[]{:S(2)}, u32[]{:S(2)}) collective-permute-start(bf16[4,2,64,768]{3,2,1,0:T(8,128)(2,1)} %get-tuple-element.28), channel_id=1, source_target_pairs={{0,16},{16,0},{1,17},{17,1},{2,18},{18,2},{3,19},{19,3},{4,20},{20... | collective-permute-start | bytes 2359304 | tf_op jit(solution)/shard_map/swap_tokens/ppermute | solution.py:122
  67.8 2.1 %collective-permute-done.2 = bf16[4,2,64,768]{3,2,1,0:T(8,128)(2,1)S(1)} collective-permute-done((bf16[4,2,64,768]{3,2,1,0:T(8,128)(2,1)}, bf16[4,2,64,768]{3,2,1,0:T(8,128)(2,1)S(1)}, u32[]{:S(2)}, u32[]{:S(2)}) %collective-permute-start.2) | collective-permute-done | bytes 786464 | tf_op jit(solution)/shard_map/swap_tokens/ppermute | solution.py:122
  69.9 0.1 broadcast_select_fusion.1
  70.0 0.1 pad_maximum_fusion
  70.1 0.1 pad_maximum_fusion.1
  70.2 13.1 %all-to-all-done.2 = bf16[16,2,16,768]{3,2,1,0:T(8,128)(2,1)S(1)} async-done(((bf16[16,2,16,768]{3,2,1,0:T(8,128)(2,1)}), bf16[16,2,16,768]{3,2,1,0:T(8,128)(2,1)S(1)}, u32[]{:S(2)}, u32[]{:S(2)}) %all-to-all-start.2) | async-done | bytes 786464 | tf_op jit(solution)/shard_map/row_sum/all_to_all | solution.py:119
  83.3 0.1 convert_reduce_fusion
  83.4 0.0 copy-start.1
  83.5 0.1 fusion.7
  83.5 17.6 %all_gather.6 = bf16[512,768]{1,0:T(8,128)(2,1)S(1)} all-gather(bf16[32,768]{1,0:T(8,128)(2,1)S(1)} %get-tuple-element.32), channel_id=1, replica_groups={{224,240,192,208,160,176,128,144,96,112,64,80,32,48,0,16},{225,241,193,..., dimensions={0}, use_global_device_ids=true | all-gather | bytes 835584 | tf_op jit(solution)/shard_map/all_gather | solution.py:140
  101.1 0.0 copy-done.1
  101.1 1.7 %convolution_convert_fusion.2 = bf16[512,768]{1,0:T(8,128)(2,1)} fusion(bf16[512,768]{1,0:T(8,128)(2,1)S(1)} %all_gather.6, bf16[768,768]{1,0:T(8,128)(2,1)S(1)} %copy-done.1), kind=kOutput, calls=%fused_computation.3 | convolution fusion | flops 604372992 | bytes 2752512 | tf_op jit(solution)/shard_map/token_sum/dot_general | solution.py:23
  102.8 8.5 %all-to-all-start.3 = ((bf16[32,16,768]{2,1,0:T(8,128)(2,1)}), bf16[32,16,768]{2,1,0:T(8,128)(2,1)S(1)}, u32[]{:S(2)}, u32[]{:S(2)}) async-start(bf16[32,16,768]{2,1,0:T(8,128)(2,1)} %bitcast.26), calls=%async_computation.3 | async-start | bytes 1572864 | tf_op jit(solution)/shard_map/token_sum/all_to_all | solution.py:145
  111.3 19.3 %all_gather.7 = bf16[512,768]{1,0:T(8,128)(2,1)S(1)} all-gather(bf16[32,768]{1,0:T(8,128)(2,1)S(1)} %get-tuple-element.19), channel_id=1, replica_groups={{224,240,192,208,160,176,128,144,96,112,64,80,32,48,0,16},{225,241,193,..., dimensions={0}, use_global_device_ids=true | all-gather | bytes 835584 | tf_op jit(solution)/shard_map/all_gather | solution.py:150
  130.6 1.8 %convolution_convert_fusion.1 = bf16[768,768]{1,0:T(8,128)(2,1)} fusion(bf16[512,768]{1,0:T(8,128)(2,1)S(1)} %bitcast.79, bf16[512,768]{1,0:T(8,128)(2,1)S(1)} %all_gather.6), kind=kOutput, calls=%fused_computation.2 | convolution fusion | flops 604569600 | bytes 2752512 | tf_op jit(solution)/shard_map/dot_general | solution.py:23
  132.4 1.8 %convolution_convert_fusion = bf16[768,768]{1,0:T(8,128)(2,1)} fusion(bf16[512,768]{1,0:T(8,128)(2,1)S(1)} %all_gather.7, bf16[512,768]{1,0:T(8,128)(2,1)S(1)} %bitcast.80), kind=kOutput, calls=%fused_computation.1 | convolution fusion | flops 604569600 | bytes 2752512 | tf_op jit(solution)/shard_map/dot_general | solution.py:23
  134.2 0.0 all-to-all-done.3
  134.2 0.7 reduce_sum.22
  (5 shorter events, 0.1 us)
Async XLA Ops:
  24.4 6.5 %copy-start = (bf16[768,768]{1,0:T(8,128)(2,1)S(1)}, bf16[768,768]{1,0:T(8,128)(2,1)}, u32[]{:S(2)}) copy-start(bf16[768,768]{1,0:T(8,128)(2,1)} %w_out.1) | copy-start | bytes 3538948
  24.4 22.9 %all-to-all-start.1 = ((bf16[4,2,2,64,768]{4,3,2,1,0:T(8,128)(2,1)}), bf16[4,2,2,64,768]{4,3,2,1,0:T(8,128)(2,1)S(1)}, u32[]{:S(2)}, u32[]{:S(2)}) async-start(bf16[4,2,2,64,768]{4,3,2,1,0:T(8,128)(2,1)} %broadcast_in_dim.15), calls=%async_computation.1 | async-start | bytes 3145728 | tf_op jit(solution)/shard_map/gather_tokens/all_to_all | solution.py:109
  28.5 18.8 %collective-permute-start = (bf16[768,768]{1,0:T(8,128)(2,1)}, bf16[768,768]{1,0:T(8,128)(2,1)}, u32[]{:S(2)}, u32[]{:S(2)}) collective-permute-start(bf16[768,768]{1,0:T(8,128)(2,1)} %w_in.1), channel_id=1, source_target_pairs={{0,16},{16,0},{1,17},{17,1},{2,18},{18,2},{3,19},{19,3},{4,20},{20... | collective-permute-start | bytes 3538952 | tf_op jit(solution)/shard_map/gather_tokens/ppermute | solution.py:112
  30.9 16.4 %collective-permute-start.1 = (bf16[768,768]{1,0:T(8,128)(2,1)S(1)}, bf16[768,768]{1,0:T(8,128)(2,1)}, u32[]{:S(2)}, u32[]{:S(2)}) collective-permute-start(bf16[768,768]{1,0:T(8,128)(2,1)S(1)} %copy-done), channel_id=1, source_target_pairs={{0,16},{16,0},{1,17},{17,1},{2,18},{18,2},{3,19},{19,3},{4,20},{20... | collective-permute-start | bytes 3538952 | tf_op jit(solution)/shard_map/gather_tokens/ppermute | solution.py:113
  51.4 31.8 %all-to-all-start.2 = ((bf16[16,2,16,768]{3,2,1,0:T(8,128)(2,1)}), bf16[16,2,16,768]{3,2,1,0:T(8,128)(2,1)S(1)}, u32[]{:S(2)}, u32[]{:S(2)}) async-start(bf16[16,2,16,768]{3,2,1,0:T(8,128)(2,1)} %chip_terms.1), calls=%async_computation.2 | async-start | bytes 1572864 | tf_op jit(solution)/shard_map/row_sum/all_to_all | solution.py:119
  65.5 4.4 %collective-permute-start.2 = (bf16[4,2,64,768]{3,2,1,0:T(8,128)(2,1)}, bf16[4,2,64,768]{3,2,1,0:T(8,128)(2,1)S(1)}, u32[]{:S(2)}, u32[]{:S(2)}) collective-permute-start(bf16[4,2,64,768]{3,2,1,0:T(8,128)(2,1)} %get-tuple-element.28), channel_id=1, source_target_pairs={{0,16},{16,0},{1,17},{17,1},{2,18},{18,2},{3,19},{19,3},{4,20},{20... | collective-permute-start | bytes 2359304 | tf_op jit(solution)/shard_map/swap_tokens/ppermute | solution.py:122
  83.4 17.7 %copy-start.1 = (bf16[768,768]{1,0:T(8,128)(2,1)S(1)}, bf16[768,768]{1,0:T(8,128)(2,1)}, u32[]{:S(2)}) copy-start(bf16[768,768]{1,0:T(8,128)(2,1)} %w_in.1) | copy-start | bytes 3538948
  102.8 31.4 %all-to-all-start.3 = ((bf16[32,16,768]{2,1,0:T(8,128)(2,1)}), bf16[32,16,768]{2,1,0:T(8,128)(2,1)S(1)}, u32[]{:S(2)}, u32[]{:S(2)}) async-start(bf16[32,16,768]{2,1,0:T(8,128)(2,1)} %bitcast.26), calls=%async_computation.3 | async-start | bytes 1572864 | tf_op jit(solution)/shard_map/token_sum/all_to_all | solution.py:145

commit v5 on v3

--- a/solution.py
+++ b/solution.py
@@ -10,6 +10,7 @@
 SIDE = ("y_hi", "y_lo", "core")
 ROW = ("z", "core")
 SWAP = [(0, 1), (1, 0)]
+SIDE_ORDER = [[2 * y + core for y in range(7, -1, -1) for core in (0, 1)]]
 ROW_ORDER = [[2 * z + core for z in range(7, -1, -1) for core in (0, 1)]]
 
 
@@ -99,10 +100,10 @@
         halves = [x.reshape(2, part, feat) for x in (inputs, out_grad)]
         own = jnp.concatenate(halves, axis=1)[None]
         own = jnp.broadcast_to(own, (8, 2, rows, feat)).reshape(16, rows, feat)
-        by_y = lax.all_to_all(own, SIDE, 0, 0, tiled=True)
+        by_y = lax.all_to_all(own, SIDE, 0, 0, axis_index_groups=SIDE_ORDER, tiled=True)
         by_y, w_in_own, w_out_own = lax.optimization_barrier((by_y, w_in, w_out))
         by_y = by_y.reshape(8, 2, 2, part, feat)
-        by_y = by_y.transpose(1, 2, 0, 3, 4).reshape(2, 2, 8 * part, feat)
+        by_y = by_y[::-1].transpose(1, 2, 0, 3, 4).reshape(2, 2, 8 * part, feat)
         by_x = jnp.broadcast_to(by_y[None], (4,) + by_y.shape)
         by_x = lax.all_to_all(by_x, "x", 0, 0, tiled=True)
         w_in_swap = lax.ppermute(w_in_own, "core", SWAP)

time: 134 us -> 133 us (level)
  blocking collectives: 60.2 us -> 58.3 us
    all_to_all x1, starting transfers between devices: 3.91 us -> 6.63 us  [body(): terms = lax.all_to_all(terms, PLANE, 0, 0, tiled=True)]
    all_to_all x1, blocking collectives: 23.9 us -> 21.6 us  [body(): lax.all_to_all(own, SIDE, 0, 0, axis_index_groups=SIDE_ORDER, tiled=True)]
    all_to_all x1, starting transfers between devices: 12.7 us -> 11.2 us  [body(): lax.all_to_all(terms, ROW, 0, 0, axis_index_groups=ROW_ORDER, tiled=True)]
where the time goes in v5:
time: 133 us
  blocking collectives  58.3 us (44%)
  waiting for transfers between devices  31.8 us (24%)
  starting transfers between devices  28.1 us (21%)
  matrix products  5.34 us (4%)
  Pallas kernels  4.13 us (3%)
  local copies, waits for them, and re-layouts  2.42 us (2%)
  other arithmetic  1.91 us (1%)
    all_to_all x1, blocking collectives, body(): lax.all_to_all(own, SIDE, 0, 0, axis_index_groups=SIDE_ORDER, tiled=True)  21.6 us
    all_gather x1, blocking collectives, body(): lax.all_gather(activation, ROW, axis_index_groups=ROW_ORDER, axis=0, tile...  19.1 us
    all_gather x1, blocking collectives, body(): lax.all_gather(pre_grad, ROW, axis_index_groups=ROW_ORDER, axis=0, tiled=...  17.6 us
    all_to_all x1, waiting for transfers between devices, body(): by_x = lax.all_to_all(by_x, 'x', 0, 0, tiled=True)  16.6 us
    all_to_all x1, waiting for transfers between devices, body(): lax.all_to_all(terms, ROW, 0, 0, axis_index_groups=ROW_ORDER, tiled=True)  13.1 us
    all_to_all x1, starting transfers between devices, body(): lax.all_to_all(terms, ROW, 0, 0, axis_index_groups=ROW_ORDER, tiled=True)  11.2 us
    all_to_all x1, starting transfers between devices, body(): terms = lax.all_to_all(terms, PLANE, 0, 0, tiled=True)  6.63 us
    dot_general x3, matrix products, dot(): lax.dot_general(left, right, (dims, ((), ())), preferred_element_type=jnp...  5.34 us
  transfers between devices with their start and end apart: 6, of which 3 were waited for; matrix products, arithmetic and copies ran while one was open for 4% of the time, Pallas kernels for 0%

profile of v5, /device:TPU:1, one launch (start us, length us, event | category | flops | bytes accessed | tf_op | source)
XLA Modules:
  0.0 132.7 jit_solution(6609495033882697332)
XLA Ops:
  0.6 0.8 pad_maximum_fusion.2
  1.4 21.6 %all_to_all.20 = bf16[16,16,768]{2,1,0:T(8,128)(2,1)S(1)} all-to-all(bf16[16,16,768]{2,1,0:T(8,128)(2,1)S(1)} %bitcast.72), channel_id=1, replica_groups={{259,275,258,274,257,273,256,272,3,19,2,18,1,17,0,16},{263,279,262,278,..., dimensions={0} | all-to-all | bytes 786432 | tf_op jit(solution)/shard_map/gather_tokens/all_to_all | solution.py:103
  23.1 1.3 broadcast_in_dim.15
  24.4 0.0 copy-start
  24.4 3.7 %all-to-all-start.1 = ((bf16[4,2,2,64,768]{4,3,2,1,0:T(8,128)(2,1)}), bf16[4,2,2,64,768]{4,3,2,1,0:T(8,128)(2,1)S(1)}, u32[]{:S(2)}, u32[]{:S(2)}) async-start(bf16[4,2,2,64,768]{4,3,2,1,0:T(8,128)(2,1)} %broadcast_in_dim.15), calls=%async_computation.1 | async-start | bytes 3145728 | tf_op jit(solution)/shard_map/gather_tokens/all_to_all | solution.py:108
  28.1 1.9 %collective-permute-start = (bf16[768,768]{1,0:T(8,128)(2,1)}, bf16[768,768]{1,0:T(8,128)(2,1)}, u32[]{:S(2)}, u32[]{:S(2)}) collective-permute-start(bf16[768,768]{1,0:T(8,128)(2,1)} %w_in.1), channel_id=1, source_target_pairs={{0,16},{16,0},{1,17},{17,1},{2,18},{18,2},{3,19},{19,3},{4,20},{20... | collective-permute-start | bytes 3538952 | tf_op jit(solution)/shard_map/gather_tokens/ppermute | solution.py:109
  30.0 0.0 copy-done
  30.0 2.4 %collective-permute-start.1 = (bf16[768,768]{1,0:T(8,128)(2,1)S(1)}, bf16[768,768]{1,0:T(8,128)(2,1)}, u32[]{:S(2)}, u32[]{:S(2)}) collective-permute-start(bf16[768,768]{1,0:T(8,128)(2,1)S(1)} %copy-done), channel_id=1, source_target_pairs={{0,16},{16,0},{1,17},{17,1},{2,18},{18,2},{3,19},{19,3},{4,20},{20... | collective-permute-start | bytes 3538952 | tf_op jit(solution)/shard_map/gather_tokens/ppermute | solution.py:110
  32.4 16.6 %all-to-all-done.1.tokens = bf16[4,2,2,64,768]{4,3,2,1,0:T(8,128)(2,1)S(1)} async-done(((bf16[4,2,2,64,768]{4,3,2,1,0:T(8,128)(2,1)}), bf16[4,2,2,64,768]{4,3,2,1,0:T(8,128)(2,1)S(1)}, u32[]{:S(2)}, u32[]{:S(2)}) %all-to-all-start.1) | async-done | bytes 1572896 | tf_op jit(solution)/shard_map/gather_tokens/all_to_all | solution.py:108
  49.0 0.0 collective-permute-done.w_in_swap
  49.0 0.0 collective-permute-done.1.w_out_swap
  49.0 4.1 %chip_terms.1 = bf16[16,2,16,768]{3,2,1,0:T(8,128)(2,1)} custom-call(s32[1]{0:T(128)} %bitcast.core, bf16[4,2,2,64,768]{4,3,2,1,0:T(8,128)(2,1)S(1)} %all-to-all-done.1.tokens, bf16[768,768]{1,0:T(8,128)(2,1)} %w_in.1, bf16[768,768]{1,0:T(8,128)(2,1)} %collective-permute-done.w_in_swap, bf16[768,768]{1,0:T(8,128)(2,1)} %w_out.1, ...), custom_call_target="tpu_custom_call" | custom-call | flops 1207959552 | bytes 4718592 | tf_op jit(solution)/shard_map/row_sum/chip_terms/pallas_call | solution.py:73
  53.1 11.2 %all-to-all-start.2 = ((bf16[16,2,16,768]{3,2,1,0:T(8,128)(2,1)}), bf16[16,2,16,768]{3,2,1,0:T(8,128)(2,1)S(1)}, u32[]{:S(2)}, u32[]{:S(2)}) async-start(bf16[16,2,16,768]{3,2,1,0:T(8,128)(2,1)} %chip_terms.1), calls=%async_computation.2 | async-start | bytes 1572864 | tf_op jit(solution)/shard_map/row_sum/all_to_all | solution.py:116
  64.3 1.0 dynamic-slice_bitcast_fusion.1
  65.3 2.3 %collective-permute-start.2 = (bf16[4,2,64,768]{3,2,1,0:T(8,128)(2,1)}, bf16[4,2,64,768]{3,2,1,0:T(8,128)(2,1)S(1)}, u32[]{:S(2)}, u32[]{:S(2)}) collective-permute-start(bf16[4,2,64,768]{3,2,1,0:T(8,128)(2,1)} %get-tuple-element.28), channel_id=1, source_target_pairs={{0,16},{16,0},{1,17},{17,1},{2,18},{18,2},{3,19},{19,3},{4,20},{20... | collective-permute-start | bytes 2359304 | tf_op jit(solution)/shard_map/swap_tokens/ppermute | solution.py:119
  67.6 2.1 %collective-permute-done.2 = bf16[4,2,64,768]{3,2,1,0:T(8,128)(2,1)S(1)} collective-permute-done((bf16[4,2,64,768]{3,2,1,0:T(8,128)(2,1)}, bf16[4,2,64,768]{3,2,1,0:T(8,128)(2,1)S(1)}, u32[]{:S(2)}, u32[]{:S(2)}) %collective-permute-start.2) | collective-permute-done | bytes 786464 | tf_op jit(solution)/shard_map/swap_tokens/ppermute | solution.py:119
  69.7 0.1 broadcast_select_fusion.1
  69.8 0.1 pad_maximum_fusion
  69.9 0.1 pad_maximum_fusion.1
  70.0 13.1 %all-to-all-done.2 = bf16[16,2,16,768]{3,2,1,0:T(8,128)(2,1)S(1)} async-done(((bf16[16,2,16,768]{3,2,1,0:T(8,128)(2,1)}), bf16[16,2,16,768]{3,2,1,0:T(8,128)(2,1)S(1)}, u32[]{:S(2)}, u32[]{:S(2)}) %all-to-all-start.2) | async-done | bytes 786464 | tf_op jit(solution)/shard_map/row_sum/all_to_all | solution.py:116
  83.1 0.1 convert_reduce_fusion
  83.2 0.0 copy-start.1
  83.2 0.1 fusion.7
  83.3 17.6 %all_gather.6 = bf16[512,768]{1,0:T(8,128)(2,1)S(1)} all-gather(bf16[32,768]{1,0:T(8,128)(2,1)S(1)} %get-tuple-element.32), channel_id=1, replica_groups={{224,240,192,208,160,176,128,144,96,112,64,80,32,48,0,16},{225,241,193,..., dimensions={0}, use_global_device_ids=true | all-gather | bytes 835584 | tf_op jit(solution)/shard_map/all_gather | solution.py:137
  100.9 0.0 copy-done.1
  100.9 1.7 %convolution_convert_fusion.2 = bf16[512,768]{1,0:T(8,128)(2,1)} fusion(bf16[512,768]{1,0:T(8,128)(2,1)S(1)} %all_gather.6, bf16[768,768]{1,0:T(8,128)(2,1)S(1)} %copy-done.1), kind=kOutput, calls=%fused_computation.3 | convolution fusion | flops 604372992 | bytes 2752512 | tf_op jit(solution)/shard_map/token_sum/dot_general | solution.py:22
  102.6 6.6 %all-to-all-start.3 = ((bf16[32,16,768]{2,1,0:T(8,128)(2,1)}), bf16[32,16,768]{2,1,0:T(8,128)(2,1)S(1)}, u32[]{:S(2)}, u32[]{:S(2)}) async-start(bf16[32,16,768]{2,1,0:T(8,128)(2,1)} %bitcast.26), calls=%async_computation.3 | async-start | bytes 1572864 | tf_op jit(solution)/shard_map/token_sum/all_to_all | solution.py:142
  109.2 19.1 %all_gather.7 = bf16[512,768]{1,0:T(8,128)(2,1)S(1)} all-gather(bf16[32,768]{1,0:T(8,128)(2,1)S(1)} %get-tuple-element.19), channel_id=1, replica_groups={{224,240,192,208,160,176,128,144,96,112,64,80,32,48,0,16},{225,241,193,..., dimensions={0}, use_global_device_ids=true | all-gather | bytes 835584 | tf_op jit(solution)/shard_map/all_gather | solution.py:145
  128.3 1.8 %convolution_convert_fusion.1 = bf16[768,768]{1,0:T(8,128)(2,1)} fusion(bf16[512,768]{1,0:T(8,128)(2,1)S(1)} %bitcast.78, bf16[512,768]{1,0:T(8,128)(2,1)S(1)} %all_gather.6), kind=kOutput, calls=%fused_computation.2 | convolution fusion | flops 604569600 | bytes 2752512 | tf_op jit(solution)/shard_map/dot_general | solution.py:22
  130.2 1.8 %convolution_convert_fusion = bf16[768,768]{1,0:T(8,128)(2,1)} fusion(bf16[512,768]{1,0:T(8,128)(2,1)S(1)} %all_gather.7, bf16[512,768]{1,0:T(8,128)(2,1)S(1)} %bitcast.79), kind=kOutput, calls=%fused_computation.1 | convolution fusion | flops 604569600 | bytes 2752512 | tf_op jit(solution)/shard_map/dot_general | solution.py:22
  132.0 0.0 all-to-all-done.3
  132.0 0.7 reduce_sum.22
  (5 shorter events, 0.1 us)
Async XLA Ops:
  24.4 5.6 %copy-start = (bf16[768,768]{1,0:T(8,128)(2,1)S(1)}, bf16[768,768]{1,0:T(8,128)(2,1)}, u32[]{:S(2)}) copy-start(bf16[768,768]{1,0:T(8,128)(2,1)} %w_out.1) | copy-start | bytes 3538948
  24.4 24.6 %all-to-all-start.1 = ((bf16[4,2,2,64,768]{4,3,2,1,0:T(8,128)(2,1)}), bf16[4,2,2,64,768]{4,3,2,1,0:T(8,128)(2,1)S(1)}, u32[]{:S(2)}, u32[]{:S(2)}) async-start(bf16[4,2,2,64,768]{4,3,2,1,0:T(8,128)(2,1)} %broadcast_in_dim.15), calls=%async_computation.1 | async-start | bytes 3145728 | tf_op jit(solution)/shard_map/gather_tokens/all_to_all | solution.py:108
  28.1 20.9 %collective-permute-start = (bf16[768,768]{1,0:T(8,128)(2,1)}, bf16[768,768]{1,0:T(8,128)(2,1)}, u32[]{:S(2)}, u32[]{:S(2)}) collective-permute-start(bf16[768,768]{1,0:T(8,128)(2,1)} %w_in.1), channel_id=1, source_target_pairs={{0,16},{16,0},{1,17},{17,1},{2,18},{18,2},{3,19},{19,3},{4,20},{20... | collective-permute-start | bytes 3538952 | tf_op jit(solution)/shard_map/gather_tokens/ppermute | solution.py:109
  30.0 19.0 %collective-permute-start.1 = (bf16[768,768]{1,0:T(8,128)(2,1)S(1)}, bf16[768,768]{1,0:T(8,128)(2,1)}, u32[]{:S(2)}, u32[]{:S(2)}) collective-permute-start(bf16[768,768]{1,0:T(8,128)(2,1)S(1)} %copy-done), channel_id=1, source_target_pairs={{0,16},{16,0},{1,17},{17,1},{2,18},{18,2},{3,19},{19,3},{4,20},{20... | collective-permute-start | bytes 3538952 | tf_op jit(solution)/shard_map/gather_tokens/ppermute | solution.py:110
  53.1 29.9 %all-to-all-start.2 = ((bf16[16,2,16,768]{3,2,1,0:T(8,128)(2,1)}), bf16[16,2,16,768]{3,2,1,0:T(8,128)(2,1)S(1)}, u32[]{:S(2)}, u32[]{:S(2)}) async-start(bf16[16,2,16,768]{3,2,1,0:T(8,128)(2,1)} %chip_terms.1), calls=%async_computation.2 | async-start | bytes 1572864 | tf_op jit(solution)/shard_map/row_sum/all_to_all | solution.py:116
  65.3 4.4 %collective-permute-start.2 = (bf16[4,2,64,768]{3,2,1,0:T(8,128)(2,1)}, bf16[4,2,64,768]{3,2,1,0:T(8,128)(2,1)S(1)}, u32[]{:S(2)}, u32[]{:S(2)}) collective-permute-start(bf16[4,2,64,768]{3,2,1,0:T(8,128)(2,1)} %get-tuple-element.28), channel_id=1, source_target_pairs={{0,16},{16,0},{1,17},{17,1},{2,18},{18,2},{3,19},{19,3},{4,20},{20... | collective-permute-start | bytes 2359304 | tf_op jit(solution)/shard_map/swap_tokens/ppermute | solution.py:119
  83.2 17.7 %copy-start.1 = (bf16[768,768]{1,0:T(8,128)(2,1)S(1)}, bf16[768,768]{1,0:T(8,128)(2,1)}, u32[]{:S(2)}) copy-start(bf16[768,768]{1,0:T(8,128)(2,1)} %w_in.1) | copy-start | bytes 3538948
  102.6 29.4 %all-to-all-start.3 = ((bf16[32,16,768]{2,1,0:T(8,128)(2,1)}), bf16[32,16,768]{2,1,0:T(8,128)(2,1)S(1)}, u32[]{:S(2)}, u32[]{:S(2)}) async-start(bf16[32,16,768]{2,1,0:T(8,128)(2,1)} %bitcast.26), calls=%async_computation.3 | async-start | bytes 1572864 | tf_op jit(solution)/shard_map/token_sum/all_to_all | solution.py:142

commit v6 on v5

--- a/solution.py
+++ b/solution.py
@@ -7,10 +7,10 @@
 from jax.sharding import PartitionSpec as P
 
 PLANE = ("x", "y_hi", "y_lo")
-SIDE = ("y_hi", "y_lo", "core")
+SIDE = ("y_hi", "y_lo")
 ROW = ("z", "core")
 SWAP = [(0, 1), (1, 0)]
-SIDE_ORDER = [[2 * y + core for y in range(7, -1, -1) for core in (0, 1)]]
+SIDE_ORDER = [list(range(7, -1, -1))]
 ROW_ORDER = [[2 * z + core for z in range(7, -1, -1) for core in (0, 1)]]
 
 
@@ -97,15 +97,16 @@
     first = core == 0
 
     with jax.named_scope("gather_tokens"):
-        halves = [x.reshape(2, part, feat) for x in (inputs, out_grad)]
-        own = jnp.concatenate(halves, axis=1)[None]
-        own = jnp.broadcast_to(own, (8, 2, rows, feat)).reshape(16, rows, feat)
+        own = jnp.concatenate([inputs, out_grad])
+        own = jnp.broadcast_to(own[None], (8,) + own.shape)
         by_y = lax.all_to_all(own, SIDE, 0, 0, axis_index_groups=SIDE_ORDER, tiled=True)
         by_y, w_in_own, w_out_own = lax.optimization_barrier((by_y, w_in, w_out))
         by_y = by_y.reshape(8, 2, 2, part, feat)
-        by_y = by_y[::-1].transpose(1, 2, 0, 3, 4).reshape(2, 2, 8 * part, feat)
+        by_y = by_y[::-1].transpose(2, 1, 0, 3, 4).reshape(2, 2, 8 * part, feat)
         by_x = jnp.broadcast_to(by_y[None], (4,) + by_y.shape)
-        by_x = lax.all_to_all(by_x, "x", 0, 0, tiled=True)
+        by_x = by_x.reshape(8, 2, 8 * part, feat)
+        by_x = lax.all_to_all(by_x, ("x", "core"), 0, 0, tiled=True)
+        by_x = by_x.reshape(4, 2, 2, 8 * part, feat)
         w_in_swap = lax.ppermute(w_in_own, "core", SWAP)
         w_out_swap = lax.ppermute(w_out_own, "core", SWAP)
         near = lax.dynamic_index_in_dim(by_x, core, 1, False)

time: 133 us -> 133 us (level)
  blocking collectives: 58.3 us -> 51.7 us
  starting transfers between devices: 28.1 us -> 34.6 us
    all_to_all x1, blocking collectives: 21.6 us -> 15.1 us  [body(): lax.all_to_all(own, SIDE, 0, 0, axis_index_groups=SIDE_ORDER, tiled=True)]
    all_to_all x1, starting transfers between devices: 3.69 us -> 9.45 us  [body(): by_x = lax.all_to_all(by_x, ('x', 'core'), 0, 0, tiled=True)]
    all_to_all x1, waiting for transfers between devices: 16.6 us -> 13.8 us  [body(): by_x = lax.all_to_all(by_x, ('x', 'core'), 0, 0, tiled=True)]
    ppermute x1, waiting for transfers between devices: 0.01 us -> 1.85 us  [body(): w_out_swap = lax.ppermute(w_out_own, 'core', SWAP)]
    all_to_all x1, starting transfers between devices: 11.2 us -> 12.5 us  [body(): lax.all_to_all(terms, ROW, 0, 0, axis_index_groups=ROW_ORDER, tiled=True)]
  transfers between devices with their start and end apart: 6 -> 6, of which waited for: 3 -> 5; matrix products, arithmetic and copies ran while one was open for 4% -> 4% of each run, Pallas kernels for 0% -> 0%
where the time goes in v6:
time: 133 us
  blocking collectives  51.7 us (39%)
  starting transfers between devices  34.6 us (26%)
  waiting for transfers between devices  31.6 us (24%)
  matrix products  5.34 us (4%)
  Pallas kernels  4.13 us (3%)
  local copies, waits for them, and re-layouts  2.42 us (2%)
  other arithmetic  1.91 us (1%)
    all_gather x1, blocking collectives, body(): lax.all_gather(activation, ROW, axis_index_groups=ROW_ORDER, axis=0, tile...  19.1 us
    all_gather x1, blocking collectives, body(): lax.all_gather(pre_grad, ROW, axis_index_groups=ROW_ORDER, axis=0, tiled=...  17.6 us
    all_to_all x1, blocking collectives, body(): lax.all_to_all(own, SIDE, 0, 0, axis_index_groups=SIDE_ORDER, tiled=True)  15.1 us
    all_to_all x1, waiting for transfers between devices, body(): by_x = lax.all_to_all(by_x, ('x', 'core'), 0, 0, tiled=True)  13.8 us
    all_to_all x1, waiting for transfers between devices, body(): lax.all_to_all(terms, ROW, 0, 0, axis_index_groups=ROW_ORDER, tiled=True)  13.1 us
    all_to_all x1, starting transfers between devices, body(): lax.all_to_all(terms, ROW, 0, 0, axis_index_groups=ROW_ORDER, tiled=True)  12.5 us
    all_to_all x1, starting transfers between devices, body(): by_x = lax.all_to_all(by_x, ('x', 'core'), 0, 0, tiled=True)  9.45 us
    all_to_all x1, starting transfers between devices, body(): terms = lax.all_to_all(terms, PLANE, 0, 0, tiled=True)  6.09 us
  transfers between devices with their start and end apart: 6, of which 5 were waited for; matrix products, arithmetic and copies ran while one was open for 4% of the time, Pallas kernels for 0%

profile of v6, /device:TPU:1, one launch (start us, length us, event | category | flops | bytes accessed | tf_op | source)
XLA Modules:
  0.0 132.5 jit_solution(8624492591810824336)
XLA Ops:
  0.6 0.8 pad_maximum_fusion.2
  1.4 15.1 %all_to_all.20 = bf16[8,32,768]{2,1,0:T(8,128)(2,1)S(1)} all-to-all(bf16[8,32,768]{2,1,0:T(8,128)(2,1)S(1)} %broadcast_in_dim.6), channel_id=1, replica_groups={{259,258,257,256,3,2,1,0},{263,262,261,260,7,6,5,4},{267,266,265,264,11..., dimensions={0} | all-to-all | bytes 786432 | tf_op jit(solution)/shard_map/gather_tokens/all_to_all | solution.py:102
  16.5 1.3 broadcast_in_dim.15
  17.8 0.0 copy-start
  17.8 9.5 %all-to-all-start.1 = ((bf16[8,2,64,768]{3,2,1,0:T(8,128)(2,1)}), bf16[8,2,64,768]{3,2,1,0:T(8,128)(2,1)S(1)}, u32[]{:S(2)}, u32[]{:S(2)}) async-start(bf16[8,2,64,768]{3,2,1,0:T(8,128)(2,1)} %bitcast.4), calls=%async_computation.1 | async-start | bytes 3145728 | tf_op jit(solution)/shard_map/gather_tokens/all_to_all | solution.py:108
  27.3 2.0 %collective-permute-start = (bf16[768,768]{1,0:T(8,128)(2,1)}, bf16[768,768]{1,0:T(8,128)(2,1)}, u32[]{:S(2)}, u32[]{:S(2)}) collective-permute-start(bf16[768,768]{1,0:T(8,128)(2,1)} %w_in.1), channel_id=1, source_target_pairs={{0,16},{16,0},{1,17},{17,1},{2,18},{18,2},{3,19},{19,3},{4,20},{20... | collective-permute-start | bytes 3538952 | tf_op jit(solution)/shard_map/gather_tokens/ppermute | solution.py:110
  29.3 0.0 copy-done
  29.3 2.3 %collective-permute-start.1 = (bf16[768,768]{1,0:T(8,128)(2,1)S(1)}, bf16[768,768]{1,0:T(8,128)(2,1)}, u32[]{:S(2)}, u32[]{:S(2)}) collective-permute-start(bf16[768,768]{1,0:T(8,128)(2,1)S(1)} %copy-done), channel_id=1, source_target_pairs={{0,16},{16,0},{1,17},{17,1},{2,18},{18,2},{3,19},{19,3},{4,20},{20... | collective-permute-start | bytes 3538952 | tf_op jit(solution)/shard_map/gather_tokens/ppermute | solution.py:111
  31.6 0.7 collective-permute-done.w_in_swap
  32.4 1.9 %collective-permute-done.1.w_out_swap = bf16[768,768]{1,0:T(8,128)(2,1)} collective-permute-done((bf16[768,768]{1,0:T(8,128)(2,1)S(1)}, bf16[768,768]{1,0:T(8,128)(2,1)}, u32[]{:S(2)}, u32[]{:S(2)}) %collective-permute-start.1) | collective-permute-done | bytes 1179680 | tf_op jit(solution)/shard_map/gather_tokens/ppermute | solution.py:111
  34.2 13.8 %all-to-all-done.1 = bf16[8,2,64,768]{3,2,1,0:T(8,128)(2,1)S(1)} async-done(((bf16[8,2,64,768]{3,2,1,0:T(8,128)(2,1)}), bf16[8,2,64,768]{3,2,1,0:T(8,128)(2,1)S(1)}, u32[]{:S(2)}, u32[]{:S(2)}) %all-to-all-start.1) | async-done | bytes 1572896 | tf_op jit(solution)/shard_map/gather_tokens/all_to_all | solution.py:108
  48.0 4.1 %chip_terms.1 = bf16[16,2,16,768]{3,2,1,0:T(8,128)(2,1)} custom-call(s32[1]{0:T(128)} %bitcast.core, bf16[4,2,2,64,768]{4,3,2,1,0:T(8,128)(2,1)S(1)} %bitcast.70, bf16[768,768]{1,0:T(8,128)(2,1)} %w_in.1, bf16[768,768]{1,0:T(8,128)(2,1)} %collective-permute-done.w_in_swap, bf16[768,768]{1,0:T(8,128)(2,1)} %w_out.1, ...), custom_call_target="tpu_custom_call" | custom-call | flops 1207959552 | bytes 4718592 | tf_op jit(solution)/shard_map/row_sum/chip_terms/pallas_call | solution.py:73
  52.2 12.5 %all-to-all-start.2 = ((bf16[16,2,16,768]{3,2,1,0:T(8,128)(2,1)}), bf16[16,2,16,768]{3,2,1,0:T(8,128)(2,1)S(1)}, u32[]{:S(2)}, u32[]{:S(2)}) async-start(bf16[16,2,16,768]{3,2,1,0:T(8,128)(2,1)} %chip_terms.1), calls=%async_computation.2 | async-start | bytes 1572864 | tf_op jit(solution)/shard_map/row_sum/all_to_all | solution.py:117
  64.6 1.0 dynamic-slice_bitcast_fusion.1
  65.7 2.3 %collective-permute-start.2 = (bf16[4,2,64,768]{3,2,1,0:T(8,128)(2,1)}, bf16[4,2,64,768]{3,2,1,0:T(8,128)(2,1)S(1)}, u32[]{:S(2)}, u32[]{:S(2)}) collective-permute-start(bf16[4,2,64,768]{3,2,1,0:T(8,128)(2,1)} %get-tuple-element.28), channel_id=1, source_target_pairs={{0,16},{16,0},{1,17},{17,1},{2,18},{18,2},{3,19},{19,3},{4,20},{20... | collective-permute-start | bytes 2359304 | tf_op jit(solution)/shard_map/swap_tokens/ppermute | solution.py:120
  67.9 2.1 %collective-permute-done.2 = bf16[4,2,64,768]{3,2,1,0:T(8,128)(2,1)S(1)} collective-permute-done((bf16[4,2,64,768]{3,2,1,0:T(8,128)(2,1)}, bf16[4,2,64,768]{3,2,1,0:T(8,128)(2,1)S(1)}, u32[]{:S(2)}, u32[]{:S(2)}) %collective-permute-start.2) | collective-permute-done | bytes 786464 | tf_op jit(solution)/shard_map/swap_tokens/ppermute | solution.py:120
  70.0 0.1 broadcast_select_fusion.1
  70.1 0.1 pad_maximum_fusion
  70.2 0.1 pad_maximum_fusion.1
  70.3 13.1 %all-to-all-done.2 = bf16[16,2,16,768]{3,2,1,0:T(8,128)(2,1)S(1)} async-done(((bf16[16,2,16,768]{3,2,1,0:T(8,128)(2,1)}), bf16[16,2,16,768]{3,2,1,0:T(8,128)(2,1)S(1)}, u32[]{:S(2)}, u32[]{:S(2)}) %all-to-all-start.2) | async-done | bytes 786464 | tf_op jit(solution)/shard_map/row_sum/all_to_all | solution.py:117
  83.4 0.1 convert_reduce_fusion
  83.5 0.0 copy-start.1
  83.6 0.1 fusion.7
  83.7 17.6 %all_gather.6 = bf16[512,768]{1,0:T(8,128)(2,1)S(1)} all-gather(bf16[32,768]{1,0:T(8,128)(2,1)S(1)} %get-tuple-element.32), channel_id=1, replica_groups={{224,240,192,208,160,176,128,144,96,112,64,80,32,48,0,16},{225,241,193,..., dimensions={0}, use_global_device_ids=true | all-gather | bytes 835584 | tf_op jit(solution)/shard_map/all_gather | solution.py:138
  101.2 0.0 copy-done.1
  101.3 1.7 %convolution_convert_fusion.2 = bf16[512,768]{1,0:T(8,128)(2,1)} fusion(bf16[512,768]{1,0:T(8,128)(2,1)S(1)} %all_gather.6, bf16[768,768]{1,0:T(8,128)(2,1)S(1)} %copy-done.1), kind=kOutput, calls=%fused_computation.3 | convolution fusion | flops 604372992 | bytes 2752512 | tf_op jit(solution)/shard_map/token_sum/dot_general | solution.py:22
  102.9 6.1 %all-to-all-start.3 = ((bf16[32,16,768]{2,1,0:T(8,128)(2,1)}), bf16[32,16,768]{2,1,0:T(8,128)(2,1)S(1)}, u32[]{:S(2)}, u32[]{:S(2)}) async-start(bf16[32,16,768]{2,1,0:T(8,128)(2,1)} %bitcast.25), calls=%async_computation.3 | async-start | bytes 1572864 | tf_op jit(solution)/shard_map/token_sum/all_to_all | solution.py:143
  109.0 19.1 %all_gather.7 = bf16[512,768]{1,0:T(8,128)(2,1)S(1)} all-gather(bf16[32,768]{1,0:T(8,128)(2,1)S(1)} %get-tuple-element.19), channel_id=1, replica_groups={{224,240,192,208,160,176,128,144,96,112,64,80,32,48,0,16},{225,241,193,..., dimensions={0}, use_global_device_ids=true | all-gather | bytes 835584 | tf_op jit(solution)/shard_map/all_gather | solution.py:146
  128.2 1.8 %convolution_convert_fusion.1 = bf16[768,768]{1,0:T(8,128)(2,1)} fusion(bf16[512,768]{1,0:T(8,128)(2,1)S(1)} %bitcast.78, bf16[512,768]{1,0:T(8,128)(2,1)S(1)} %all_gather.6), kind=kOutput, calls=%fused_computation.2 | convolution fusion | flops 604569600 | bytes 2752512 | tf_op jit(solution)/shard_map/dot_general | solution.py:22
  130.0 1.8 %convolution_convert_fusion = bf16[768,768]{1,0:T(8,128)(2,1)} fusion(bf16[512,768]{1,0:T(8,128)(2,1)S(1)} %all_gather.7, bf16[512,768]{1,0:T(8,128)(2,1)S(1)} %bitcast.79), kind=kOutput, calls=%fused_computation.1 | convolution fusion | flops 604569600 | bytes 2752512 | tf_op jit(solution)/shard_map/dot_general | solution.py:22
  131.8 0.0 all-to-all-done.3
  131.8 0.7 reduce_sum.22
  (5 shorter events, 0.1 us)
Async XLA Ops:
  17.8 11.5 %copy-start = (bf16[768,768]{1,0:T(8,128)(2,1)S(1)}, bf16[768,768]{1,0:T(8,128)(2,1)}, u32[]{:S(2)}) copy-start(bf16[768,768]{1,0:T(8,128)(2,1)} %w_out.1) | copy-start | bytes 3538948
  17.8 30.2 %all-to-all-start.1 = ((bf16[8,2,64,768]{3,2,1,0:T(8,128)(2,1)}), bf16[8,2,64,768]{3,2,1,0:T(8,128)(2,1)S(1)}, u32[]{:S(2)}, u32[]{:S(2)}) async-start(bf16[8,2,64,768]{3,2,1,0:T(8,128)(2,1)} %bitcast.4), calls=%async_computation.1 | async-start | bytes 3145728 | tf_op jit(solution)/shard_map/gather_tokens/all_to_all | solution.py:108
  27.3 5.1 %collective-permute-start = (bf16[768,768]{1,0:T(8,128)(2,1)}, bf16[768,768]{1,0:T(8,128)(2,1)}, u32[]{:S(2)}, u32[]{:S(2)}) collective-permute-start(bf16[768,768]{1,0:T(8,128)(2,1)} %w_in.1), channel_id=1, source_target_pairs={{0,16},{16,0},{1,17},{17,1},{2,18},{18,2},{3,19},{19,3},{4,20},{20... | collective-permute-start | bytes 3538952 | tf_op jit(solution)/shard_map/gather_tokens/ppermute | solution.py:110
  29.3 4.9 %collective-permute-start.1 = (bf16[768,768]{1,0:T(8,128)(2,1)S(1)}, bf16[768,768]{1,0:T(8,128)(2,1)}, u32[]{:S(2)}, u32[]{:S(2)}) collective-permute-start(bf16[768,768]{1,0:T(8,128)(2,1)S(1)} %copy-done), channel_id=1, source_target_pairs={{0,16},{16,0},{1,17},{17,1},{2,18},{18,2},{3,19},{19,3},{4,20},{20... | collective-permute-start | bytes 3538952 | tf_op jit(solution)/shard_map/gather_tokens/ppermute | solution.py:111
  52.2 31.3 %all-to-all-start.2 = ((bf16[16,2,16,768]{3,2,1,0:T(8,128)(2,1)}), bf16[16,2,16,768]{3,2,1,0:T(8,128)(2,1)S(1)}, u32[]{:S(2)}, u32[]{:S(2)}) async-start(bf16[16,2,16,768]{3,2,1,0:T(8,128)(2,1)} %chip_terms.1), calls=%async_computation.2 | async-start | bytes 1572864 | tf_op jit(solution)/shard_map/row_sum/all_to_all | solution.py:117
  65.7 4.4 %collective-permute-start.2 = (bf16[4,2,64,768]{3,2,1,0:T(8,128)(2,1)}, bf16[4,2,64,768]{3,2,1,0:T(8,128)(2,1)S(1)}, u32[]{:S(2)}, u32[]{:S(2)}) collective-permute-start(bf16[4,2,64,768]{3,2,1,0:T(8,128)(2,1)} %get-tuple-element.28), channel_id=1, source_target_pairs={{0,16},{16,0},{1,17},{17,1},{2,18},{18,2},{3,19},{19,3},{4,20},{20... | collective-permute-start | bytes 2359304 | tf_op jit(solution)/shard_map/swap_tokens/ppermute | solution.py:120
  83.5 17.7 %copy-start.1 = (bf16[768,768]{1,0:T(8,128)(2,1)S(1)}, bf16[768,768]{1,0:T(8,128)(2,1)}, u32[]{:S(2)}) copy-start(bf16[768,768]{1,0:T(8,128)(2,1)} %w_in.1) | copy-start | bytes 3538948
  102.9 28.9 %all-to-all-start.3 = ((bf16[32,16,768]{2,1,0:T(8,128)(2,1)}), bf16[32,16,768]{2,1,0:T(8,128)(2,1)S(1)}, u32[]{:S(2)}, u32[]{:S(2)}) async-start(bf16[32,16,768]{2,1,0:T(8,128)(2,1)} %bitcast.25), calls=%async_computation.3 | async-start | bytes 1572864 | tf_op jit(solution)/shard_map/token_sum/all_to_all | solution.py:143

commit v7 on v6

--- a/solution.py
+++ b/solution.py
@@ -24,68 +24,81 @@
     ).astype(out)
 
 
-def terms_kernel(core, tokens, w_in, w_in_swap, w_out, w_out_swap, terms, up, down, sems):
-    near, far = core[0], 1 - core[0]
-    blocks, _, feat, block = up.shape
-    count = tokens.shape[0] * tokens.shape[3]
-
-    def fetches(j):
-        span = pl.ds(j * block, block)
-        pairs = (
-            (w_in.at[:, span], up.at[j, 0]),
-            (w_in_swap.at[:, span], up.at[j, 1]),
-            (w_out.at[span, :], down.at[j, 0]),
-            (w_out_swap.at[span, :], down.at[j, 1]),
-        )
-        return [
-            pltpu.make_async_copy(source, target, sems.at[j, k])
-            for k, (source, target) in enumerate(pairs)
-        ]
-
-    for j in range(blocks):
-        for fetch in fetches(j):
-            fetch.start()
-
-    def lhs(side, kind):
-        return tokens[:, side, kind].reshape(count, feat)
-
-    for j in range(blocks):
-        for fetch in fetches(j):
-            fetch.wait()
-        pre = dot(lhs(near, 0), up[j, 0], ((1,), (0,)))
-        pre += dot(lhs(far, 0), up[j, 1], ((1,), (0,)))
-        back = dot(lhs(near, 1), down[j, 0], ((1,), (1,)))
-        back += dot(lhs(far, 1), down[j, 1], ((1,), (1,)))
-        for kind, value in enumerate((pre, back)):
-            terms[:, kind, :, pl.ds(j * block, block)] = value.astype(terms.dtype).reshape(
-                16, count // 16, block
-            )
+def stage_kernel(weight, held, sem):
+    copy = pltpu.make_async_copy(weight, held, sem)
+    copy.start()
+    copy.wait()
 
 
-def chip_terms(core, tokens, *weights):
-    feat, hid = weights[0].shape
-    weights = [pltpu.with_memory_space_constraint(w, pltpu.HBM) for w in weights]
+def stage_weight(weight):
+    return pl.pallas_call(
+        stage_kernel,
+        in_specs=[pl.BlockSpec(memory_space=pltpu.HBM)],
+        out_specs=pl.BlockSpec(memory_space=pltpu.VMEM),
+        out_shape=pltpu.VMEM(weight.shape, weight.dtype),
+        scratch_shapes=[pltpu.SemaphoreType.DMA],
+        compiler_params=pltpu.CompilerParams(vmem_limit_bytes=8 * 1024 * 1024),
+        cost_estimate=pl.CostEstimate(
+            flops=0, bytes_accessed=4 * weight.size, transcendentals=0
+        ),
+        name="stage_weight",
+    )(pltpu.with_memory_space_constraint(weight, pltpu.HBM))
+
+
+def terms_kernel(core, tokens, up, down, far_up, far_down, terms, held, total, sems):
+    near, far = core[0], 1 - core[0]
+    share, hid = terms.shape[2:]
+    feat = tokens.shape[4]
     block = 256
-    blocks = hid // block
+    fetches = [
+        pltpu.make_async_copy(source, held.at[k], sems.at[k])
+        for k, source in enumerate((down, far_up, far_down))
+    ]
+    for fetch in fetches:
+        fetch.start()
+
+    def product(side, kind, weights, span):
+        left = tokens[:, side, kind].reshape(16 * share, feat)
+        if kind == 0:
+            return dot(left, weights[:, span], ((1,), (0,)))
+        return dot(left, weights[span, :], ((1,), (1,)))
+
+    spans = [pl.ds(j * block, block) for j in range(hid // block)]
+    for span in spans:
+        total[0, :, span] = product(near, 0, up, span)
+    for fetch in fetches:
+        fetch.wait()
+    for span in spans:
+        total[1, :, span] = product(near, 1, held.at[0], span)
+    for kind in (0, 1):
+        for span in spans:
+            value = total[kind, :, span] + product(far, kind, held.at[1 + kind], span)
+            terms[:, kind, :, span] = value.astype(terms.dtype).reshape(16, share, block)
+
+
+def chip_terms(core, tokens, up, down, far_up, far_down):
+    feat, hid = up.shape
     count = tokens.shape[0] * tokens.shape[3]
+    up = pltpu.with_memory_space_constraint(up, pltpu.VMEM)
+    rest = [pltpu.with_memory_space_constraint(w, pltpu.HBM) for w in (down, far_up, far_down)]
     far = pl.BlockSpec(memory_space=pltpu.HBM)
     near = pl.BlockSpec(memory_space=pltpu.VMEM)
     return pl.pallas_call(
         terms_kernel,
-        in_specs=[pl.BlockSpec(memory_space=pltpu.SMEM), near, far, far, far, far],
+        in_specs=[pl.BlockSpec(memory_space=pltpu.SMEM), near, near, far, far, far],
         out_specs=near,
         out_shape=jax.ShapeDtypeStruct((16, 2, count // 16, hid), jnp.bfloat16),
         scratch_shapes=[
-            pltpu.VMEM((blocks, 2, feat, block), jnp.bfloat16),
-            pltpu.VMEM((blocks, 2, block, feat), jnp.bfloat16),
-            pltpu.SemaphoreType.DMA((blocks, 4)),
+            pltpu.VMEM((3, feat, hid), jnp.bfloat16),
+            pltpu.VMEM((2, count, hid), jnp.float32),
+            pltpu.SemaphoreType.DMA((3,)),
         ],
         compiler_params=pltpu.CompilerParams(vmem_limit_bytes=32 * 1024 * 1024),
         cost_estimate=pl.CostEstimate(
             flops=8 * count * feat * hid, bytes_accessed=8 * feat * hid, transcendentals=0
         ),
         name="chip_terms",
-    )(core, tokens, *weights)
+    )(core, tokens, up, *rest)
 
 
 def body(inputs, out_grad, w_in, w_out):
@@ -113,7 +126,8 @@
         far = lax.dynamic_index_in_dim(by_x, 1 - core, 1, False)
 
     with jax.named_scope("row_sum"):
-        terms = chip_terms(core.reshape(1), by_x, w_in, w_in_swap, w_out, w_out_swap)
+        up = stage_weight(w_in_own)
+        terms = chip_terms(core.reshape(1), by_x, up, w_out, w_in_swap, w_out_swap)
         terms = lax.all_to_all(terms, ROW, 0, 0, axis_index_groups=ROW_ORDER, tiled=True)
 
     with jax.named_scope("swap_tokens"):

time: 133 us -> 134 us (level)
  Pallas kernels: 4.13 us -> 5.52 us
  transfers between devices with their start and end apart: 6 -> 6, of which waited for: 5 -> 4; matrix products, arithmetic and copies ran while one was open for 4% -> 4% of each run, Pallas kernels for 0% -> 1%
where the time goes in v7:
time: 134 us
  blocking collectives  51.6 us (39%)
  starting transfers between devices  34.5 us (26%)
  waiting for transfers between devices  30.3 us (23%)
  matrix products  6.6 us (5%)
  Pallas kernels  5.52 us (4%)
  local copies, waits for them, and re-layouts  2.41 us (2%)
  other arithmetic  1.91 us (1%)
    all_gather x1, blocking collectives, body(): lax.all_gather(activation, ROW, axis_index_groups=ROW_ORDER, axis=0, tile...  19.1 us
    all_gather x1, blocking collectives, body(): lax.all_gather(pre_grad, ROW, axis_index_groups=ROW_ORDER, axis=0, tiled=...  17.4 us
    all_to_all x1, blocking collectives, body(): lax.all_to_all(own, SIDE, 0, 0, axis_index_groups=SIDE_ORDER, tiled=True)  15.1 us
    all_to_all x1, waiting for transfers between devices, body(): by_x = lax.all_to_all(by_x, ('x', 'core'), 0, 0, tiled=True)  13.6 us
    all_to_all x1, waiting for transfers between devices, body(): lax.all_to_all(terms, ROW, 0, 0, axis_index_groups=ROW_ORDER, tiled=True)  13.1 us
    all_to_all x1, starting transfers between devices, body(): lax.all_to_all(terms, ROW, 0, 0, axis_index_groups=ROW_ORDER, tiled=True)  12.5 us
    all_to_all x1, starting transfers between devices, body(): by_x = lax.all_to_all(by_x, ('x', 'core'), 0, 0, tiled=True)  9.32 us
    dot_general x3, matrix products, dot(): lax.dot_general(left, right, (dims, ((), ())), preferred_element_type=jnp...  6.6 us
  transfers between devices with their start and end apart: 6, of which 4 were waited for; matrix products, arithmetic and copies ran while one was open for 4% of the time, Pallas kernels for 1%

profile of v7, /device:TPU:1, one launch (start us, length us, event | category | flops | bytes accessed | tf_op | source)
XLA Modules:
  0.0 133.6 jit_solution(12865386652538866211)
XLA Ops:
  0.6 0.8 pad_maximum_fusion.2
  1.4 15.1 %all_to_all.20 = bf16[8,32,768]{2,1,0:T(8,128)(2,1)S(1)} all-to-all(bf16[8,32,768]{2,1,0:T(8,128)(2,1)S(1)} %broadcast_in_dim.6), channel_id=1, replica_groups={{259,258,257,256,3,2,1,0},{263,262,261,260,7,6,5,4},{267,266,265,264,11..., dimensions={0} | all-to-all | bytes 786432 | tf_op jit(solution)/shard_map/gather_tokens/all_to_all | solution.py:115
  16.5 1.3 broadcast_in_dim.15
  17.8 9.3 %all-to-all-start.1 = ((bf16[8,2,64,768]{3,2,1,0:T(8,128)(2,1)}), bf16[8,2,64,768]{3,2,1,0:T(8,128)(2,1)S(1)}, u32[]{:S(2)}, u32[]{:S(2)}) async-start(bf16[8,2,64,768]{3,2,1,0:T(8,128)(2,1)} %bitcast.4), calls=%async_computation.1 | async-start | bytes 3145728 | tf_op jit(solution)/shard_map/gather_tokens/all_to_all | solution.py:121
  27.2 2.0 %collective-permute-start = (bf16[768,768]{1,0:T(8,128)(2,1)}, bf16[768,768]{1,0:T(8,128)(2,1)}, u32[]{:S(2)}, u32[]{:S(2)}) collective-permute-start(bf16[768,768]{1,0:T(8,128)(2,1)} %weight), channel_id=1, source_target_pairs={{0,16},{16,0},{1,17},{17,1},{2,18},{18,2},{3,19},{19,3},{4,20},{20... | collective-permute-start | bytes 3538952 | tf_op jit(solution)/shard_map/gather_tokens/ppermute | solution.py:123
  29.2 2.3 %collective-permute-start.1 = (bf16[768,768]{1,0:T(8,128)(2,1)}, bf16[768,768]{1,0:T(8,128)(2,1)}, u32[]{:S(2)}, u32[]{:S(2)}) collective-permute-start(bf16[768,768]{1,0:T(8,128)(2,1)} %down.1), channel_id=1, source_target_pairs={{0,16},{16,0},{1,17},{17,1},{2,18},{18,2},{3,19},{19,3},{4,20},{20... | collective-permute-start | bytes 3538952 | tf_op jit(solution)/shard_map/gather_tokens/ppermute | solution.py:124
  31.5 1.3 stage_weight.1.up
  32.8 0.0 collective-permute-done.far_up
  32.8 1.5 %collective-permute-done.1.far_down = bf16[768,768]{1,0:T(8,128)(2,1)} collective-permute-done((bf16[768,768]{1,0:T(8,128)(2,1)}, bf16[768,768]{1,0:T(8,128)(2,1)}, u32[]{:S(2)}, u32[]{:S(2)}) %collective-permute-start.1) | collective-permute-done | bytes 1179680 | tf_op jit(solution)/shard_map/gather_tokens/ppermute | solution.py:124
  34.3 13.6 %all-to-all-done.1 = bf16[8,2,64,768]{3,2,1,0:T(8,128)(2,1)S(1)} async-done(((bf16[8,2,64,768]{3,2,1,0:T(8,128)(2,1)}), bf16[8,2,64,768]{3,2,1,0:T(8,128)(2,1)S(1)}, u32[]{:S(2)}, u32[]{:S(2)}) %all-to-all-start.1) | async-done | bytes 1572896 | tf_op jit(solution)/shard_map/gather_tokens/all_to_all | solution.py:121
  47.9 4.2 %chip_terms.1 = bf16[16,2,16,768]{3,2,1,0:T(8,128)(2,1)} custom-call(s32[1]{0:T(128)} %bitcast.core, bf16[4,2,2,64,768]{4,3,2,1,0:T(8,128)(2,1)S(1)} %bitcast.70, bf16[768,768]{1,0:T(8,128)(2,1)S(1)} %stage_weight.1.up, bf16[768,768]{1,0:T(8,128)(2,1)} %down.1, bf16[768,768]{1,0:T(8,128)(2,1)} %collective-permute-done.far_up, ...), custom_call_target="tpu_custom_call" | custom-call | flops 1207959552 | bytes 4718592 | tf_op jit(solution)/shard_map/row_sum/chip_terms/pallas_call | solution.py:86
  52.1 12.5 %all-to-all-start.2 = ((bf16[16,2,16,768]{3,2,1,0:T(8,128)(2,1)}), bf16[16,2,16,768]{3,2,1,0:T(8,128)(2,1)S(1)}, u32[]{:S(2)}, u32[]{:S(2)}) async-start(bf16[16,2,16,768]{3,2,1,0:T(8,128)(2,1)} %chip_terms.1), calls=%async_computation.2 | async-start | bytes 1572864 | tf_op jit(solution)/shard_map/row_sum/all_to_all | solution.py:131
  64.6 1.0 dynamic-slice_bitcast_fusion.1
  65.6 2.3 %collective-permute-start.2 = (bf16[4,2,64,768]{3,2,1,0:T(8,128)(2,1)}, bf16[4,2,64,768]{3,2,1,0:T(8,128)(2,1)S(1)}, u32[]{:S(2)}, u32[]{:S(2)}) collective-permute-start(bf16[4,2,64,768]{3,2,1,0:T(8,128)(2,1)} %get-tuple-element.28), channel_id=1, source_target_pairs={{0,16},{16,0},{1,17},{17,1},{2,18},{18,2},{3,19},{19,3},{4,20},{20... | collective-permute-start | bytes 2359304 | tf_op jit(solution)/shard_map/swap_tokens/ppermute | solution.py:134
  67.9 2.1 %collective-permute-done.2 = bf16[4,2,64,768]{3,2,1,0:T(8,128)(2,1)S(1)} collective-permute-done((bf16[4,2,64,768]{3,2,1,0:T(8,128)(2,1)}, bf16[4,2,64,768]{3,2,1,0:T(8,128)(2,1)S(1)}, u32[]{:S(2)}, u32[]{:S(2)}) %collective-permute-start.2) | collective-permute-done | bytes 786464 | tf_op jit(solution)/shard_map/swap_tokens/ppermute | solution.py:134
  70.0 0.1 broadcast_select_fusion.1
  70.1 0.1 pad_maximum_fusion
  70.2 0.1 pad_maximum_fusion.1
  70.3 13.1 %all-to-all-done.2 = bf16[16,2,16,768]{3,2,1,0:T(8,128)(2,1)S(1)} async-done(((bf16[16,2,16,768]{3,2,1,0:T(8,128)(2,1)}), bf16[16,2,16,768]{3,2,1,0:T(8,128)(2,1)S(1)}, u32[]{:S(2)}, u32[]{:S(2)}) %all-to-all-start.2) | async-done | bytes 786464 | tf_op jit(solution)/shard_map/row_sum/all_to_all | solution.py:131
  83.4 0.1 convert_reduce_fusion
  83.6 0.1 fusion.7
  83.7 17.4 %all_gather.6 = bf16[512,768]{1,0:T(8,128)(2,1)S(1)} all-gather(bf16[32,768]{1,0:T(8,128)(2,1)S(1)} %get-tuple-element.32), channel_id=1, replica_groups={{224,240,192,208,160,176,128,144,96,112,64,80,32,48,0,16},{225,241,193,..., dimensions={0}, use_global_device_ids=true | all-gather | bytes 835584 | tf_op jit(solution)/shard_map/all_gather | solution.py:152
  101.1 3.0 %convolution_convert_fusion.2 = bf16[512,768]{1,0:T(8,128)(2,1)} fusion(bf16[512,768]{1,0:T(8,128)(2,1)S(1)} %all_gather.6, bf16[768,768]{1,0:T(8,128)(2,1)} %weight), kind=kOutput, calls=%fused_computation.3 | convolution fusion | flops 604372992 | bytes 2752512 | tf_op jit(solution)/shard_map/token_sum/dot_general | solution.py:22
  104.0 6.1 %all-to-all-start.3 = ((bf16[32,16,768]{2,1,0:T(8,128)(2,1)}), bf16[32,16,768]{2,1,0:T(8,128)(2,1)S(1)}, u32[]{:S(2)}, u32[]{:S(2)}) async-start(bf16[32,16,768]{2,1,0:T(8,128)(2,1)} %bitcast.25), calls=%async_computation.3 | async-start | bytes 1572864 | tf_op jit(solution)/shard_map/token_sum/all_to_all | solution.py:157
  110.1 19.1 %all_gather.7 = bf16[512,768]{1,0:T(8,128)(2,1)S(1)} all-gather(bf16[32,768]{1,0:T(8,128)(2,1)S(1)} %get-tuple-element.19), channel_id=1, replica_groups={{224,240,192,208,160,176,128,144,96,112,64,80,32,48,0,16},{225,241,193,..., dimensions={0}, use_global_device_ids=true | all-gather | bytes 835584 | tf_op jit(solution)/shard_map/all_gather | solution.py:160
  129.3 1.8 %convolution_convert_fusion.1 = bf16[768,768]{1,0:T(8,128)(2,1)} fusion(bf16[512,768]{1,0:T(8,128)(2,1)S(1)} %bitcast.78, bf16[512,768]{1,0:T(8,128)(2,1)S(1)} %all_gather.6), kind=kOutput, calls=%fused_computation.2 | convolution fusion | flops 604569600 | bytes 2752512 | tf_op jit(solution)/shard_map/dot_general | solution.py:22
  131.1 1.8 %convolution_convert_fusion = bf16[768,768]{1,0:T(8,128)(2,1)} fusion(bf16[512,768]{1,0:T(8,128)(2,1)S(1)} %all_gather.7, bf16[512,768]{1,0:T(8,128)(2,1)S(1)} %bitcast.79), kind=kOutput, calls=%fused_computation.1 | convolution fusion | flops 604569600 | bytes 2752512 | tf_op jit(solution)/shard_map/dot_general | solution.py:22
  132.9 0.0 all-to-all-done.3
  132.9 0.7 reduce_sum.22
  (5 shorter events, 0.1 us)
Async XLA Ops:
  17.8 30.1 %all-to-all-start.1 = ((bf16[8,2,64,768]{3,2,1,0:T(8,128)(2,1)}), bf16[8,2,64,768]{3,2,1,0:T(8,128)(2,1)S(1)}, u32[]{:S(2)}, u32[]{:S(2)}) async-start(bf16[8,2,64,768]{3,2,1,0:T(8,128)(2,1)} %bitcast.4), calls=%async_computation.1 | async-start | bytes 3145728 | tf_op jit(solution)/shard_map/gather_tokens/all_to_all | solution.py:121
  27.2 5.6 %collective-permute-start = (bf16[768,768]{1,0:T(8,128)(2,1)}, bf16[768,768]{1,0:T(8,128)(2,1)}, u32[]{:S(2)}, u32[]{:S(2)}) collective-permute-start(bf16[768,768]{1,0:T(8,128)(2,1)} %weight), channel_id=1, source_target_pairs={{0,16},{16,0},{1,17},{17,1},{2,18},{18,2},{3,19},{19,3},{4,20},{20... | collective-permute-start | bytes 3538952 | tf_op jit(solution)/shard_map/gather_tokens/ppermute | solution.py:123
  29.2 5.1 %collective-permute-start.1 = (bf16[768,768]{1,0:T(8,128)(2,1)}, bf16[768,768]{1,0:T(8,128)(2,1)}, u32[]{:S(2)}, u32[]{:S(2)}) collective-permute-start(bf16[768,768]{1,0:T(8,128)(2,1)} %down.1), channel_id=1, source_target_pairs={{0,16},{16,0},{1,17},{17,1},{2,18},{18,2},{3,19},{19,3},{4,20},{20... | collective-permute-start | bytes 3538952 | tf_op jit(solution)/shard_map/gather_tokens/ppermute | solution.py:124
  52.1 31.3 %all-to-all-start.2 = ((bf16[16,2,16,768]{3,2,1,0:T(8,128)(2,1)}), bf16[16,2,16,768]{3,2,1,0:T(8,128)(2,1)S(1)}, u32[]{:S(2)}, u32[]{:S(2)}) async-start(bf16[16,2,16,768]{3,2,1,0:T(8,128)(2,1)} %chip_terms.1), calls=%async_computation.2 | async-start | bytes 1572864 | tf_op jit(solution)/shard_map/row_sum/all_to_all | solution.py:131
  65.6 4.4 %collective-permute-start.2 = (bf16[4,2,64,768]{3,2,1,0:T(8,128)(2,1)}, bf16[4,2,64,768]{3,2,1,0:T(8,128)(2,1)S(1)}, u32[]{:S(2)}, u32[]{:S(2)}) collective-permute-start(bf16[4,2,64,768]{3,2,1,0:T(8,128)(2,1)} %get-tuple-element.28), channel_id=1, source_target_pairs={{0,16},{16,0},{1,17},{17,1},{2,18},{18,2},{3,19},{19,3},{4,20},{20... | collective-permute-start | bytes 2359304 | tf_op jit(solution)/shard_map/swap_tokens/ppermute | solution.py:134
  104.0 28.9 %all-to-all-start.3 = ((bf16[32,16,768]{2,1,0:T(8,128)(2,1)}), bf16[32,16,768]{2,1,0:T(8,128)(2,1)S(1)}, u32[]{:S(2)}, u32[]{:S(2)}) async-start(bf16[32,16,768]{2,1,0:T(8,128)(2,1)} %bitcast.25), calls=%async_computation.3 | async-start | bytes 1572864 | tf_op jit(solution)/shard_map/token_sum/all_to_all | solution.py:157
